TPU v7x, 32 devices: a whole 2x2x4 slice. The times are simulated.
32 devices in a mesh: sky: 2 (over x), tm: 16 (over z, y, core).
Axes of the slice: x: 2, y: 2, z: 4, core: 2. Of those that a mesh axis runs over, the one named last changes fastest.
Arguments:
- series: bfloat16 [4, 4, 1024, 2048], P('sky', None, 'tm'), parts along dimension 0, may hold values from -6 to 6
- antenna: float32 [4, 3], P('sky'), parts along dimension 0, as said below
- offsets: int32 [16, 2], P('sky'), parts along dimension 0, may hold values from -8 to 8, as said below
Outputs:
- detection: float32 [16, 1024, 2048], P('sky', 'tm'), parts along dimension 0
There are 2 independent parts, one for each index of `sky`. A program takes and returns all parts, laid end to end along the dimension named above; each array names one. Nothing has to cross between parts.
Inputs may be any that keep to these rules, and one draw needn't show every extreme that they name: `offsets`: both -8 and 8 occur in every draw. `antenna`: A and B are positive and C C is at most 0.49 A B in every row.
All inputs are finite; a program needn't handle non-finite values.
Results may differ from a plain program's by a relative error of at most 0.0032.
Values may be sent and summed in bfloat16 or wider, within the bound.
No kernel may reach another device: no remote copies, remote signals or barrier semaphores. Data moves between devices by JAX's collectives and lax.ppermute only.
A program may use at most 128 MiB of HBM per device.

v0:
```python
import functools
import math

import jax
import jax.numpy as jnp
import numpy as np
from jax import lax
from jax.experimental import pallas as pl
from jax.experimental.pallas import tpu as pltpu
from jax.sharding import PartitionSpec as P

DMAX = 8
LANES = 128
BF16 = jnp.bfloat16
F32 = jnp.float32
SEG, LOWEST, TOP, FIRST, LAST = range(5)
SMEM = pl.BlockSpec(memory_space=pltpu.SMEM)
VMEM = pl.BlockSpec(memory_space=pltpu.VMEM)
ANY = pl.BlockSpec(memory_space=pl.ANY)


def params(mebibytes):
    return pltpu.CompilerParams(vmem_limit_bytes=mebibytes * 1024 * 1024)


def cost(flops, moved):
    return pl.CostEstimate(flops=flops, bytes_accessed=moved, transcendentals=0)


def dft_table(rows, cols, length):
    products = rows[:, None].astype(np.int64) * cols[None, :] % length
    angle = products.astype(np.float32) * np.float32(2.0 * math.pi / length)
    return np.cos(angle), -np.sin(angle)


def in_hbm(x):
    return pltpu.with_memory_space_constraint(x, pltpu.HBM)


def dot(x, y):
    return jnp.dot(x, y, preferred_element_type=F32)


def pack_kernel(x_ref, out_ref):
    cols = out_ref.shape[-1]
    for piece in range(out_ref.shape[0]):
        out_ref[piece] = x_ref[0, :, :, piece * cols : (piece + 1) * cols]


def pack(series, groups):
    segs, comps, rows, width = series.shape
    shape = (segs * groups, comps, rows, width // groups)
    return pl.pallas_call(
        pack_kernel,
        grid=(segs,),
        in_specs=[pl.BlockSpec((1, comps, rows, width), lambda s: (s, 0, 0, 0))],
        out_specs=pl.BlockSpec((groups,) + shape[1:], lambda s: (s, 0, 0, 0)),
        out_shape=pltpu.HBM(shape, BF16),
        compiler_params=params(16),
        cost_estimate=cost(0, 4 * math.prod(shape)),
        name="pack",
    )(in_hbm(series))


def first_kernel(half_ref, x_ref, wr_ref, wi_ref, br_ref, bi_ref, vr_ref, vi_ref, out_ref):
    length = wr_ref.shape[1]
    cols = x_ref.shape[-1]
    shape = (out_ref.shape[0],) + out_ref.shape[2:]
    by_real, by_imag = vr_ref[...], vi_ref[...]
    t_real = br_ref[...] * by_real - bi_ref[...] * by_imag
    t_imag = br_ref[...] * by_imag + bi_ref[...] * by_real
    for lead in range(0, x_ref.shape[1], 2):
        x_real = x_ref[:, lead].reshape(length, cols)
        x_imag = x_ref[:, lead + 1].reshape(length, cols)
        real_part = dot(wr_ref[...], x_real) - dot(wi_ref[...], x_imag)
        imag_part = dot(wi_ref[...], x_real) + dot(wr_ref[...], x_imag)
        out_ref[:, lead] = (real_part * t_real - imag_part * t_imag).astype(BF16).reshape(shape)
        out_ref[:, lead + 1] = (real_part * t_imag + imag_part * t_real).astype(BF16).reshape(shape)


def first_pass(pieces, half, tables, bases, turns, groups):
    count, comps, rows, cols = pieces.shape
    length = count * rows
    per_half = groups * rows
    tile = min(256, per_half)
    steps = per_half // tile
    strip = lambda width: pl.BlockSpec((tile, width), lambda t, half: (half[0] * steps + t, 0))
    return pl.pallas_call(
        first_kernel,
        grid_spec=pltpu.PrefetchScalarGridSpec(
            num_scalar_prefetch=1,
            grid=(steps,),
            in_specs=[pl.BlockSpec(pieces.shape, lambda t, half: (0, 0, 0, 0))]
            + [strip(length)] * 2
            + [strip(cols)] * 2
            + [strip(1)] * 2,
            out_specs=pl.BlockSpec((tile // rows, comps, rows, cols), lambda t, half: (t, 0, 0, 0)),
        ),
        out_shape=pltpu.HBM((groups, comps, rows, cols), BF16),
        compiler_params=params(20),
        cost_estimate=cost(4 * comps * per_half * length * cols, 4 * per_half * length),
        name="first_pass",
    )(half, pieces, *map(in_hbm, tables), *map(in_hbm, bases), *turns)


def gather_rows(z_ref, lhs_ref):
    groups, _, _, cols = z_ref.shape
    height = lhs_ref.shape[0] // 2
    odd = lax.broadcasted_iota(jnp.int32, (height, cols), 1) % 2 == 1
    for source in range(groups):
        at = slice(source * cols, (source + 1) * cols)
        piece = z_ref[source].reshape(height, cols)
        lhs_ref[:height, at] = piece
        lhs_ref[height:, at] = jnp.where(odd, -piece, piece)


def fstat_kernel(coef_ref, z_ref, wr_ref, wi_ref, *refs):
    fstat_ref, tail_ref, head_ref, lhs_ref = refs[-4:]
    step = pl.program_id(0)

    @pl.when(step == 0)
    def _():
        gather_rows(z_ref, lhs_ref)

    rows, width = fstat_ref.shape
    tile = wr_ref.shape[1]
    by_real = dot(lhs_ref[...], wr_ref[...])
    by_imag = dot(lhs_ref[...], wi_ref[...])
    for half in range(2):
        part = lambda x, comp: x[(4 * half + comp) * rows : (4 * half + comp + 1) * rows]
        a_real = part(by_real, 0) - part(by_imag, 1)
        a_imag = part(by_imag, 0) + part(by_real, 1)
        b_real = part(by_real, 2) - part(by_imag, 3)
        b_imag = part(by_imag, 2) + part(by_real, 3)
        fstat = (
            coef_ref[1] * (a_real * a_real + a_imag * a_imag)
            + coef_ref[0] * (b_real * b_real + b_imag * b_imag)
            - coef_ref[2] * (a_real * b_real + a_imag * b_imag)
        )
        begin = pl.multiple_of(step * tile, tile)
        rims = pl.ds(half * DMAX, DMAX), pl.ds(begin, tile)
        tail_ref[rims] = fstat[rows - DMAX :]
        head_ref[rims] = fstat[:DMAX]
        at = pl.ds(pl.multiple_of(half * (width // 2) + begin, tile), tile)
        fstat_ref[:, at] = fstat.astype(fstat_ref.dtype)


def fstat_pass(z, tables, coefs, kind, after=()):
    groups, comps, rows, cols = z.shape
    width = groups * cols
    span = width // 2
    tile = min(256, span)
    rim = (2 * DMAX, span)
    still = lambda shape: pl.BlockSpec(shape, lambda t: (0,) * len(shape))
    return pl.pallas_call(
        fstat_kernel,
        grid=(span // tile,),
        in_specs=[SMEM, still(z.shape)] + [pl.BlockSpec((width, tile), lambda t: (0, t))] * 2 + [ANY] * len(after),
        out_specs=[still((rows, width)), still(rim), still(rim)],
        out_shape=[jax.ShapeDtypeStruct((rows, width), kind)] + [jax.ShapeDtypeStruct(rim, F32)] * 2,
        scratch_shapes=[pltpu.VMEM((2 * comps * rows, width), BF16)],
        compiler_params=params(24),
        cost_estimate=cost(4 * comps * rows * width * width, 2 * width * width),
        name="fstat_pass",
    )(coefs, z, *map(in_hbm, tables), *after)


def detect_kernel(offsets_ref, place_ref, other_ref, own_ref, *refs):
    early_refs, late_refs, out_ref, wide_refs = refs[:2], refs[2:4], refs[4], refs[5:]
    rows = own_ref.shape[0]

    @pl.when(pl.program_id(0) == 0)
    def _():
        is_first, is_last, seg = place_ref[FIRST] == 1, place_ref[LAST] == 1, place_ref[SEG]
        lowest, top = place_ref[LOWEST] == 1, place_ref[TOP] == 1
        width = own_ref.shape[1]
        unfold = lambda ref: jnp.concatenate([ref[:DMAX], ref[DMAX:]], axis=1)
        early, late = [unfold(ref) for ref in early_refs], [unfold(ref) for ref in late_refs]

        def widen(wide_ref, middle, lower, upper):
            lower = jnp.where(is_first, pltpu.roll(lower, 1, 1), lower)
            upper = jnp.where(is_last, pltpu.roll(upper, width - 1, 1), upper)
            for strip in range(width // LANES):
                at = slice(strip * LANES, (strip + 1) * LANES)
                wide_ref[strip, :DMAX] = lower[:, at]
                wide_ref[strip, DMAX : DMAX + rows] = middle[:, at]
                wide_ref[strip, DMAX + rows :] = upper[:, at]

        def place(own_wide, other_wide):
            lower = jnp.where(lowest, early[0], late[0]), jnp.where(lowest, late[0], early[0])
            upper = jnp.where(top, early[1], late[1]), jnp.where(top, late[1], early[1])
            widen(own_wide, own_ref[...], lower[0], upper[0])
            widen(other_wide, other_ref[...].astype(F32), lower[1], upper[1])

        @pl.when(seg == 0)
        def _():
            place(wide_refs[0], wide_refs[1])

        @pl.when(seg != 0)
        def _():
            place(wide_refs[1], wide_refs[0])

    template = pl.program_id(0)
    begins = [DMAX + offsets_ref[template, s] for s in range(len(wide_refs))]
    for strip in range(own_ref.shape[1] // LANES):
        total = wide_refs[0][strip, pl.ds(begins[0], rows), :]
        for begin, wide_ref in zip(begins[1:], wide_refs[1:]):
            total = total + wide_ref[strip, pl.ds(begin, rows), :]
        out_ref[0, :, strip * LANES : (strip + 1) * LANES] = total * (1.0 / len(wide_refs))


def detect(offsets, place, other, own, early, late):
    templates = offsets.shape[0]
    rows, width = own.shape
    return pl.pallas_call(
        detect_kernel,
        grid=(templates,),
        in_specs=[SMEM, SMEM] + [VMEM] * 6,
        out_specs=pl.BlockSpec((1, rows, width), lambda t: (t, 0, 0)),
        out_shape=jax.ShapeDtypeStruct((templates, rows, width), F32),
        scratch_shapes=[pltpu.VMEM((width // LANES, rows + 2 * DMAX, LANES), F32)] * 2,
        compiler_params=params(8),
        cost_estimate=cost(3 * templates * rows * width, 4 * templates * rows * width),
        name="detect",
    )(offsets, place, other, own, *early, *late)


def local(series, antenna, offsets):
    devices = lax.axis_size("tm")
    index = lax.axis_index("tm")
    segs, _, rows, width = series.shape
    slow = devices * rows
    length = slow * width
    groups = devices // segs
    cols = width // groups
    seg, member = index // groups, index % groups
    place = jnp.stack([seg, member == 0, member == groups - 1, index == 0, index == devices - 1]).astype(jnp.int32)

    bins = np.arange(slow)
    short = [x.astype(BF16) for x in dft_table(bins, bins, slow)]
    long = [x.astype(BF16) for x in dft_table(np.arange(width), np.arange(width // 2), width)]
    bases = dft_table(bins, np.arange(cols), length)
    angle = (jnp.arange(slow, dtype=jnp.int32) * (member * cols) % length).astype(F32) * (2.0 * math.pi / length)
    turns = (jnp.cos(angle)[:, None], -jnp.sin(angle)[:, None])
    coef = lax.dynamic_index_in_dim(antenna, seg, 0, keepdims=False)
    scale = (coef[0] * coef[1] - coef[2] * coef[2]) * length
    coefs = coef * jnp.array([1.0, 1.0, 2.0], F32) / scale

    halves = [[g * groups + i for i in range(groups)] for g in range(segs)]
    trade = functools.partial(lax.all_to_all, axis_name="tm", split_axis=0, concat_axis=0, tiled=True)
    pieces = trade(pack(series, groups))

    def rows_of(half):
        turned = first_pass(pieces, half[None], short, bases, turns, groups)
        return trade(turned, axis_index_groups=halves)

    def move(x, by):
        return lax.ppermute(x, "tm", [(i, (i + by) % devices) for i in range(devices)])

    far, near = rows_of(1 - seg), rows_of(seg)
    other, tail, head = fstat_pass(far, long, coefs, BF16)
    other = move(other, groups)
    early = [move(tail, groups + 1), move(head, groups - 1)]
    own, tail, head = fstat_pass(near, long, coefs, F32, early)
    late = [move(tail, 1), move(head, -1)]
    return detect(offsets, place, other, own, early, late)


def solution(mesh):
    return jax.shard_map(
        local,
        mesh=mesh,
        in_specs=(P("sky", None, "tm", None), P("sky", None), P("sky", None)),
        out_specs=P("sky", "tm", None),
        check_vma=False,
    )
```

profile of v0, /device:TPU:0, one launch (start us, length us, event | category | flops | bytes accessed | tf_op | source)
XLA Modules:
  0.0 129.5 jit_solution(6294135204448384726)
XLA Ops:
  0.0 2.6 %pack.1 = bf16[16,4,64,256]{3,2,1,0:T(8,128)(2,1)} custom-call(bf16[2,4,64,2048]{3,2,1,0:T(8,128)(2,1)} %x_ref.1), custom_call_target="tpu_custom_call" | custom-call | bytes 4194304 | tf_op jit(solution)/shard_map/pack/pallas_call | solution.py:53
  2.6 7.4 %all-to-all-start = ((bf16[16,4,64,256]{3,2,1,0:T(8,128)(2,1)}), bf16[16,4,64,256]{3,2,1,0:T(8,128)(2,1)S(1)}, u32[]{:S(2)}, u32[]{:S(2)}) async-start(bf16[16,4,64,256]{3,2,1,0:T(8,128)(2,1)} %pack.1), calls=%async_computation | async-start | bytes 4194304 | tf_op jit(solution)/shard_map/all_to_all | solution.py:251
  10.1 1.0 copy.12
  11.1 2.8 %sine_negate_fusion = (f32[1024,1]{1,0:T(8,128)S(1)}, f32[1024,1]{1,0:T(8,128)S(1)}) fusion(f32[1024,1]{1,0:T(8,128)} %copy.12), kind=kLoop, calls=%fused_computation | loop fusion | flops 2048 | bytes 12288 | tf_op jit(solution)/shard_map/neg | solution.py:244
  13.9 37.2 %all-to-all-done.x_ref = bf16[16,4,64,256]{3,2,1,0:T(8,128)(2,1)S(1)} async-done(((bf16[16,4,64,256]{3,2,1,0:T(8,128)(2,1)}), bf16[16,4,64,256]{3,2,1,0:T(8,128)(2,1)S(1)}, u32[]{:S(2)}, u32[]{:S(2)}) %all-to-all-start) | async-done | bytes 2097184 | tf_op jit(solution)/shard_map/all_to_all | solution.py:251
  51.1 4.9 %first_pass.2 = bf16[8,4,64,256]{3,2,1,0:T(8,128)(2,1)} custom-call(s32[1]{0:T(128)} %bitcast.7.half_ref, bf16[16,4,64,256]{3,2,1,0:T(8,128)(2,1)S(1)} %all-to-all-done.x_ref, bf16[1024,1024]{1,0:T(8,128)(2,1)} %constant.76.clone.wr_ref, bf16[1024,1024]{1,0:T(8,128)(2,1)} %constant.77.clone.wi_ref, f32[1024,256]{1,0:T(8,128)} %constant.78.clone.br_ref, ...), custom_call_target="tpu_custom_call" | custom-call | flops 2147483648 | bytes 2097152 | tf_op jit(solution)/shard_map/first_pass/pallas_call | solution.py:88
  56.0 10.3 %all-to-all-start.1 = ((bf16[8,4,64,256]{3,2,1,0:T(8,128)(2,1)}), bf16[8,4,64,256]{3,2,1,0:T(8,128)(2,1)}, u32[]{:S(2)}, u32[]{:S(2)}) async-start(bf16[8,4,64,256]{3,2,1,0:T(8,128)(2,1)} %first_pass.2), calls=%async_computation.1 | async-start | bytes 2097152 | tf_op jit(solution)/shard_map/all_to_all | solution.py:255
  66.3 4.9 %first_pass.3 = bf16[8,4,64,256]{3,2,1,0:T(8,128)(2,1)} custom-call(s32[1]{0:T(128)} %bitcast.half_ref, bf16[16,4,64,256]{3,2,1,0:T(8,128)(2,1)S(1)} %all-to-all-done.x_ref, bf16[1024,1024]{1,0:T(8,128)(2,1)} %constant.76.clone.wr_ref, bf16[1024,1024]{1,0:T(8,128)(2,1)} %constant.77.clone.wi_ref, f32[1024,256]{1,0:T(8,128)} %constant.78.clone.br_ref, ...), custom_call_target="tpu_custom_call" | custom-call | flops 2147483648 | bytes 2097152 | tf_op jit(solution)/shard_map/first_pass/pallas_call | solution.py:88
  71.2 0.0 copy-start.2
  71.2 0.0 copy-start.1
  71.2 9.6 %all-to-all-done.1.z_ref = bf16[8,4,64,256]{3,2,1,0:T(8,128)(2,1)} async-done(((bf16[8,4,64,256]{3,2,1,0:T(8,128)(2,1)}), bf16[8,4,64,256]{3,2,1,0:T(8,128)(2,1)}, u32[]{:S(2)}, u32[]{:S(2)}) %all-to-all-start.1) | async-done | bytes 1048608 | tf_op jit(solution)/shard_map/all_to_all | solution.py:255
  80.8 3.6 %all-to-all-start.2 = ((bf16[8,4,64,256]{3,2,1,0:T(8,128)(2,1)}), bf16[8,4,64,256]{3,2,1,0:T(8,128)(2,1)S(1)}, u32[]{:S(2)}, u32[]{:S(2)}) async-start(bf16[8,4,64,256]{3,2,1,0:T(8,128)(2,1)} %first_pass.3), calls=%async_computation.2 | async-start | bytes 2097152 | tf_op jit(solution)/shard_map/all_to_all | solution.py:255
  84.4 0.0 copy-done.2
  84.4 0.7 fusion.2
  87.6 0.0 copy-done.1
  87.7 7.6 %fstat_pass.2 = (bf16[64,2048]{1,0:T(8,128)(2,1)S(1)}, f32[16,1024]{1,0:T(8,128)S(1)}, f32[16,1024]{1,0:T(8,128)S(1)}) custom-call(f32[3]{0:T(128)S(1)} %divide_bitcast_fusion.coef_ref, bf16[8,4,64,256]{3,2,1,0:T(8,128)(2,1)} %all-to-all-done.1.z_ref, bf16[2048,1024]{1,0:T(8,128)(2,1)} %constant.80.clone.wr_ref, bf16[2048,1024]{1,0:T(8,128)(2,1)} %constant.81.clone.wi_ref), custom_call_target="tpu_custom_call" | custom-call | flops 4294967296 | bytes 8388608 | tf_op jit(solution)/shard_map/fstat_pass/pallas_call | solution.py:155
  95.3 3.3 %collective-permute-start.1 = (f32[16,1024]{1,0:T(8,128)S(1)}, f32[16,1024]{1,0:T(8,128)S(1)}, u32[]{:S(2)}, u32[]{:S(2)}) collective-permute-start(f32[16,1024]{1,0:T(8,128)S(1)} %get-tuple-element.12), channel_id=1, source_target_pairs={{0,9},{1,10},{2,11},{3,12},{4,13},{5,14},{6,15},{7,0},{8,1},{9,2},... | collective-permute-start | bytes 196616 | tf_op jit(solution)/shard_map/ppermute | solution.py:258
  98.6 0.0 collective-permute-start.2
  98.6 2.7 %collective-permute-start = (bf16[64,2048]{1,0:T(8,128)(2,1)S(1)}, bf16[64,2048]{1,0:T(8,128)(2,1)S(1)}, u32[]{:S(2)}, u32[]{:S(2)}) collective-permute-start(bf16[64,2048]{1,0:T(8,128)(2,1)S(1)} %get-tuple-element.11), channel_id=1, source_target_pairs={{0,8},{1,9},{2,10},{3,11},{4,12},{5,13},{6,14},{7,15},{8,0},{9,1},... | collective-permute-start | bytes 786440 | tf_op jit(solution)/shard_map/ppermute | solution.py:258
  101.3 0.0 all-to-all-done.2.z_ref
  101.3 0.0 collective-permute-done.1.refs_0_
  101.3 10.0 %collective-permute-done.2.refs_1_ = f32[16,1024]{1,0:T(8,128)S(1)} collective-permute-done((f32[16,1024]{1,0:T(8,128)S(1)}, f32[16,1024]{1,0:T(8,128)S(1)}, u32[]{:S(2)}, u32[]{:S(2)}) %collective-permute-start.2) | collective-permute-done | bytes 65568 | tf_op jit(solution)/shard_map/ppermute | solution.py:258
  111.2 7.3 %fstat_pass.3 = (f32[64,2048]{1,0:T(8,128)S(1)}, f32[16,1024]{1,0:T(8,128)S(1)}, f32[16,1024]{1,0:T(8,128)S(1)}) custom-call(f32[3]{0:T(128)S(1)} %divide_bitcast_fusion.coef_ref, bf16[8,4,64,256]{3,2,1,0:T(8,128)(2,1)S(1)} %all-to-all-done.2.z_ref, bf16[2048,1024]{1,0:T(8,128)(2,1)} %constant.80.clone.wr_ref, bf16[2048,1024]{1,0:T(8,128)(2,1)} %constant.81.clone.wi_ref, ...), custom_call_target="tpu_custom_call" | custom-call | flops 4294967296 | bytes 8388608 | tf_op jit(solution)/shard_map/fstat_pass/pallas_call | solution.py:155
  118.5 1.7 %collective-permute-start.3 = (f32[16,1024]{1,0:T(8,128)S(1)}, f32[16,1024]{1,0:T(8,128)S(1)}, u32[]{:S(2)}, u32[]{:S(2)}) collective-permute-start(f32[16,1024]{1,0:T(8,128)S(1)} %get-tuple-element.15), channel_id=1, source_target_pairs={{0,1},{1,2},{2,3},{3,4},{4,5},{5,6},{6,7},{7,8},{8,9},{9,10},{10,1... | collective-permute-start | bytes 196616 | tf_op jit(solution)/shard_map/ppermute | solution.py:258
  120.2 2.8 %collective-permute-start.4 = (f32[16,1024]{1,0:T(8,128)S(1)}, f32[16,1024]{1,0:T(8,128)S(1)}, u32[]{:S(2)}, u32[]{:S(2)}) collective-permute-start(f32[16,1024]{1,0:T(8,128)S(1)} %get-tuple-element.16), channel_id=1, source_target_pairs={{0,15},{1,0},{2,1},{3,2},{4,3},{5,4},{6,5},{7,6},{8,7},{9,8},{10,9... | collective-permute-start | bytes 196616 | tf_op jit(solution)/shard_map/ppermute | solution.py:258
  123.0 0.0 copy-done
  123.0 0.1 copy.13.offsets_ref
  123.1 0.1 stack.39.place_ref
  123.2 1.8 %collective-permute-done.3.refs_2_ = f32[16,1024]{1,0:T(8,128)S(1)} collective-permute-done((f32[16,1024]{1,0:T(8,128)S(1)}, f32[16,1024]{1,0:T(8,128)S(1)}, u32[]{:S(2)}, u32[]{:S(2)}) %collective-permute-start.3) | collective-permute-done | bytes 65568 | tf_op jit(solution)/shard_map/ppermute | solution.py:258
  125.0 0.0 collective-permute-done.4.refs_3_
  125.0 0.0 collective-permute-done.other_ref
  125.0 4.5 %detect.1 = f32[8,64,2048]{2,1,0:T(8,128)} custom-call(s32[8,2]{1,0:T(8,128)S(1)} %copy.13.offsets_ref, s32[5]{0:T(128)S(1)} %stack.39.place_ref, bf16[64,2048]{1,0:T(8,128)(2,1)S(1)} %collective-permute-done.other_ref, f32[64,2048]{1,0:T(8,128)S(1)} %get-tuple-element.14.own_ref, f32[16,1024]{1,0:T(8,128)S(1)} %collective-permute-done.1.refs_0_, ...), custom_call_target="tpu_custom_call" | custom-call | flops 3145728 | bytes 4194304 | tf_op jit(solution)/shard_map/detect/pallas_call | solution.py:215
  (4 shorter events, 0.0 us)
Async XLA Ops:
  2.6 48.5 %all-to-all-start = ((bf16[16,4,64,256]{3,2,1,0:T(8,128)(2,1)}), bf16[16,4,64,256]{3,2,1,0:T(8,128)(2,1)S(1)}, u32[]{:S(2)}, u32[]{:S(2)}) async-start(bf16[16,4,64,256]{3,2,1,0:T(8,128)(2,1)} %pack.1), calls=%async_computation | async-start | bytes 4194304 | tf_op jit(solution)/shard_map/all_to_all | solution.py:251
  56.0 24.8 %all-to-all-start.1 = ((bf16[8,4,64,256]{3,2,1,0:T(8,128)(2,1)}), bf16[8,4,64,256]{3,2,1,0:T(8,128)(2,1)}, u32[]{:S(2)}, u32[]{:S(2)}) async-start(bf16[8,4,64,256]{3,2,1,0:T(8,128)(2,1)} %first_pass.2), calls=%async_computation.1 | async-start | bytes 2097152 | tf_op jit(solution)/shard_map/all_to_all | solution.py:255
  71.2 13.2 %copy-start.2 = (f32[2,3]{1,0:T(2,128)S(1)}, f32[2,3]{1,0:T(2,128)}, u32[]{:S(2)}) copy-start(f32[2,3]{1,0:T(2,128)} %param.11) | copy-start | bytes 76
  71.2 16.4 %copy-start.1 = (f32[1,3]{1,0:T(1,128)S(1)}, f32[1,3]{1,0:T(1,128)}, u32[]{:S(2)}) copy-start(f32[1,3]{1,0:T(1,128)} %constant.82) | copy-start | bytes 40
  80.8 20.4 %all-to-all-start.2 = ((bf16[8,4,64,256]{3,2,1,0:T(8,128)(2,1)}), bf16[8,4,64,256]{3,2,1,0:T(8,128)(2,1)S(1)}, u32[]{:S(2)}, u32[]{:S(2)}) async-start(bf16[8,4,64,256]{3,2,1,0:T(8,128)(2,1)} %first_pass.3), calls=%async_computation.2 | async-start | bytes 2097152 | tf_op jit(solution)/shard_map/all_to_all | solution.py:255
  95.3 6.0 %collective-permute-start.1 = (f32[16,1024]{1,0:T(8,128)S(1)}, f32[16,1024]{1,0:T(8,128)S(1)}, u32[]{:S(2)}, u32[]{:S(2)}) collective-permute-start(f32[16,1024]{1,0:T(8,128)S(1)} %get-tuple-element.12), channel_id=1, source_target_pairs={{0,9},{1,10},{2,11},{3,12},{4,13},{5,14},{6,15},{7,0},{8,1},{9,2},... | collective-permute-start | bytes 196616 | tf_op jit(solution)/shard_map/ppermute | solution.py:258
  98.6 12.7 %collective-permute-start.2 = (f32[16,1024]{1,0:T(8,128)S(1)}, f32[16,1024]{1,0:T(8,128)S(1)}, u32[]{:S(2)}, u32[]{:S(2)}) collective-permute-start(f32[16,1024]{1,0:T(8,128)S(1)} %get-tuple-element.13), channel_id=1, source_target_pairs={{0,7},{1,8},{2,9},{3,10},{4,11},{5,12},{6,13},{7,14},{8,15},{9,0},... | collective-permute-start | bytes 196616 | tf_op jit(solution)/shard_map/ppermute | solution.py:258
  98.6 24.4 %copy-start = (s32[8,2]{0,1:T(2,128)S(1)}, s32[8,2]{0,1:T(2,128)}, u32[]{:S(2)}) copy-start(s32[8,2]{0,1:T(2,128)} %param.12) | copy-start | bytes 196
  98.6 26.4 %collective-permute-start = (bf16[64,2048]{1,0:T(8,128)(2,1)S(1)}, bf16[64,2048]{1,0:T(8,128)(2,1)S(1)}, u32[]{:S(2)}, u32[]{:S(2)}) collective-permute-start(bf16[64,2048]{1,0:T(8,128)(2,1)S(1)} %get-tuple-element.11), channel_id=1, source_target_pairs={{0,8},{1,9},{2,10},{3,11},{4,12},{5,13},{6,14},{7,15},{8,0},{9,1},... | collective-permute-start | bytes 786440 | tf_op jit(solution)/shard_map/ppermute | solution.py:258
  118.5 6.4 %collective-permute-start.3 = (f32[16,1024]{1,0:T(8,128)S(1)}, f32[16,1024]{1,0:T(8,128)S(1)}, u32[]{:S(2)}, u32[]{:S(2)}) collective-permute-start(f32[16,1024]{1,0:T(8,128)S(1)} %get-tuple-element.15), channel_id=1, source_target_pairs={{0,1},{1,2},{2,3},{3,4},{4,5},{5,6},{6,7},{7,8},{8,9},{9,10},{10,1... | collective-permute-start | bytes 196616 | tf_op jit(solution)/shard_map/ppermute | solution.py:258
  120.2 4.7 %collective-permute-start.4 = (f32[16,1024]{1,0:T(8,128)S(1)}, f32[16,1024]{1,0:T(8,128)S(1)}, u32[]{:S(2)}, u32[]{:S(2)}) collective-permute-start(f32[16,1024]{1,0:T(8,128)S(1)} %get-tuple-element.16), channel_id=1, source_target_pairs={{0,15},{1,0},{2,1},{3,2},{4,3},{5,4},{6,5},{7,6},{8,7},{9,8},{10,9... | collective-permute-start | bytes 196616 | tf_op jit(solution)/shard_map/ppermute | solution.py:258
where the time goes:
time: 130 us; the launch traced here: 129 us
  waiting for transfers between devices  58.6 us (45%)
  Pallas kernels  31.8 us (24%)
  starting transfers between devices  31.7 us (24%)
  other arithmetic  2.86 us (2%)
  between operations  2.65 us (2%)
  local copies, waits for them, and re-layouts  1.86 us (1%)
    all_to_all x1, waiting for transfers between devices, local(): pieces = trade(pack(series, groups))  37.2 us
    pallas_call x2, Pallas kernels, fstat_pass(): pl.pallas_call(fstat_kernel, grid=(span // tile,), in_specs=[SMEM, still(...  14.9 us
    all_to_all x2, starting transfers between devices, rows_of(): return trade(turned, axis_index_groups=halves)  13.8 us
    ppermute x5, waiting for transfers between devices, move(): lax.ppermute(x, 'tm', [(i, (i + by) % devices) for i in range(devices)])  11.8 us
    ppermute x5, starting transfers between devices, move(): lax.ppermute(x, 'tm', [(i, (i + by) % devices) for i in range(devices)])  10.4 us
    pallas_call x2, Pallas kernels, first_pass(): pl.pallas_call(first_kernel, grid_spec=pltpu.PrefetchScalarGridSpec(num_s...  9.83 us
    all_to_all x2, waiting for transfers between devices, rows_of(): return trade(turned, axis_index_groups=halves)  9.62 us
    all_to_all x1, starting transfers between devices, local(): pieces = trade(pack(series, groups))  7.39 us
  transfers between devices with their start and end apart: 8, of which 4 were waited for; matrix products, arithmetic and copies ran while one was open for 4% of the time, Pallas kernels for 15%

commit v1 on v0

v1 whole, which is shorter than its diff:
```python
import functools
import math

import jax
import jax.numpy as jnp
import numpy as np
from jax import lax
from jax.experimental import pallas as pl
from jax.experimental.pallas import tpu as pltpu
from jax.sharding import PartitionSpec as P

DMAX = 8
LANES = 128
BF16 = jnp.bfloat16
F32 = jnp.float32
SEG, LOWEST, TOP, FIRST, LAST = range(5)
SMEM = pl.BlockSpec(memory_space=pltpu.SMEM)
VMEM = pl.BlockSpec(memory_space=pltpu.VMEM)
ANY = pl.BlockSpec(memory_space=pl.ANY)


def params(mebibytes):
    return pltpu.CompilerParams(vmem_limit_bytes=mebibytes * 1024 * 1024)


def cost(flops, moved):
    return pl.CostEstimate(flops=flops, bytes_accessed=moved, transcendentals=0)


def dft_table(rows, cols, length):
    products = rows[:, None].astype(np.int64) * cols[None, :] % length
    angle = products.astype(np.float32) * np.float32(2.0 * math.pi / length)
    return np.cos(angle), -np.sin(angle)


def in_hbm(x):
    return pltpu.with_memory_space_constraint(x, pltpu.HBM)


def dot(x, y):
    return jnp.dot(x, y, preferred_element_type=F32)


def pack_kernel(x_ref, out_ref):
    cols = out_ref.shape[-1]
    for piece in range(out_ref.shape[0]):
        out_ref[piece] = x_ref[0, :, :, piece * cols : (piece + 1) * cols]


def pack(series, groups):
    segs, comps, rows, width = series.shape
    shape = (segs * groups, comps, rows, width // groups)
    return pl.pallas_call(
        pack_kernel,
        grid=(segs,),
        in_specs=[pl.BlockSpec((1, comps, rows, width), lambda s: (s, 0, 0, 0))],
        out_specs=pl.BlockSpec((groups,) + shape[1:], lambda s: (s, 0, 0, 0)),
        out_shape=pltpu.HBM(shape, BF16),
        compiler_params=params(16),
        cost_estimate=cost(0, 4 * math.prod(shape)),
        name="pack",
    )(in_hbm(series))


def first_kernel(x_ref, sort_ref, wr_ref, wi_ref, br_ref, bi_ref, vr_ref, vi_ref, out_ref, sorted_ref):
    length = wr_ref.shape[1]
    comps, cols = x_ref.shape[1], x_ref.shape[-1]

    @pl.when(pl.program_id(0) == 0)
    def _():
        for comp in range(comps):
            sorted_ref[comp] = dot(x_ref[:, comp].reshape(length, cols), sort_ref[...]).astype(BF16)

    shape = (out_ref.shape[0],) + out_ref.shape[3:]
    by_real, by_imag = vr_ref[...], vi_ref[...]
    t_real = br_ref[...] * by_real - bi_ref[...] * by_imag
    t_imag = br_ref[...] * by_imag + bi_ref[...] * by_real
    for lead in range(0, comps, 2):
        x_real, x_imag = sorted_ref[lead], sorted_ref[lead + 1]
        real_part = dot(wr_ref[...], x_real) - dot(wi_ref[...], x_imag)
        imag_part = dot(wi_ref[...], x_real) + dot(wr_ref[...], x_imag)
        out_ref[:, 0, lead] = (real_part * t_real - imag_part * t_imag).astype(BF16).reshape(shape)
        out_ref[:, 0, lead + 1] = (real_part * t_imag + imag_part * t_real).astype(BF16).reshape(shape)


def first_pass(pieces, order, tables, bases, turns, groups):
    count, comps, rows, cols = pieces.shape
    length = count * rows
    segs = count // groups
    tile = min(256, groups * rows)
    steps = groups * rows // tile
    sort = np.zeros((cols, cols), np.float32)
    sort[order, np.arange(cols)] = 1.0
    strip = lambda width: pl.BlockSpec((tile, width), lambda t: (t, 0))
    return pl.pallas_call(
        first_kernel,
        grid=(segs * steps,),
        in_specs=[
            pl.BlockSpec(pieces.shape, lambda t: (0, 0, 0, 0)),
            pl.BlockSpec((cols, cols), lambda t: (0, 0)),
        ]
        + [strip(length)] * 2
        + [strip(cols)] * 2
        + [strip(1)] * 2,
        out_specs=pl.BlockSpec((tile // rows, 1, comps, rows, cols), lambda t: (t % steps, t // steps, 0, 0, 0)),
        out_shape=pltpu.HBM((groups, segs, comps, rows, cols), BF16),
        scratch_shapes=[pltpu.VMEM((comps, length, cols), BF16)],
        compiler_params=params(24),
        cost_estimate=cost(4 * comps * length * length * cols, 4 * length * length),
        name="first_pass",
    )(pieces, in_hbm(sort.astype(BF16)), *map(in_hbm, tables), *map(in_hbm, bases), *turns)


def fstat_kernel(half_ref, coef_ref, z_ref, er_ref, ei_ref, or_ref, oi_ref, fstat_ref, tail_ref, head_ref, lhs_ref):
    step = pl.program_id(0)

    @pl.when(step == 0)
    def _():
        groups, cols = z_ref.shape[0], z_ref.shape[-1] // 2
        for source in range(groups):
            piece = z_ref[source, 0].reshape(lhs_ref.shape[1], 2 * cols)
            for parity in range(2):
                at = slice(source * cols, (source + 1) * cols)
                lhs_ref[parity, :, at] = piece[:, parity * cols : (parity + 1) * cols]

    rows, width = fstat_ref.shape
    tile = er_ref.shape[1]
    even, odd = lhs_ref[0], lhs_ref[1]
    even_real, even_imag = dot(even, er_ref[...]), dot(even, ei_ref[...])
    odd_real, odd_imag = dot(odd, or_ref[...]), dot(odd, oi_ref[...])
    tails, heads = [], []
    for half in range(2):
        by_real = even_real - odd_real if half else even_real + odd_real
        by_imag = even_imag - odd_imag if half else even_imag + odd_imag
        part = lambda x, comp: x[comp * rows : (comp + 1) * rows]
        a_real = part(by_real, 0) - part(by_imag, 1)
        a_imag = part(by_imag, 0) + part(by_real, 1)
        b_real = part(by_real, 2) - part(by_imag, 3)
        b_imag = part(by_imag, 2) + part(by_real, 3)
        fstat = (
            coef_ref[1] * (a_real * a_real + a_imag * a_imag)
            + coef_ref[0] * (b_real * b_real + b_imag * b_imag)
            - coef_ref[2] * (a_real * b_real + a_imag * b_imag)
        )
        tails.append(fstat[rows - DMAX :])
        heads.append(fstat[:DMAX])
        at = pl.ds(pl.multiple_of(half * (width // 2) + step * tile, tile), tile)
        fstat_ref[:, at] = fstat.astype(fstat_ref.dtype)
    at = pl.ds(pl.multiple_of(step * tile, tile), tile)
    tail_ref[:, at] = jnp.concatenate(tails, axis=0).astype(tail_ref.dtype)
    head_ref[:, at] = jnp.concatenate(heads, axis=0).astype(head_ref.dtype)


def fstat_pass(z, half, tables, coefs, kind):
    groups, _, comps, rows, cols = z.shape
    width = groups * cols
    span = width // 2
    tile = min(256, span)
    rim = (2 * DMAX, span)
    still = lambda shape: pl.BlockSpec(shape, lambda t, half: (0,) * len(shape))
    return pl.pallas_call(
        fstat_kernel,
        grid_spec=pltpu.PrefetchScalarGridSpec(
            num_scalar_prefetch=1,
            grid=(span // tile,),
            in_specs=[SMEM, pl.BlockSpec((groups, 1, comps, rows, cols), lambda t, half: (0, half[0], 0, 0, 0))]
            + [pl.BlockSpec((span, tile), lambda t, half: (0, t))] * 4,
            out_specs=[still((rows, width)), still(rim), still(rim)],
            scratch_shapes=[pltpu.VMEM((2, comps * rows, span), BF16)],
        ),
        out_shape=[jax.ShapeDtypeStruct((rows, width), kind)] + [jax.ShapeDtypeStruct(rim, kind)] * 2,
        compiler_params=params(24),
        cost_estimate=cost(2 * comps * rows * width * width, 2 * width * width),
        name="fstat_pass",
    )(half, coefs, z, *map(in_hbm, tables))


def detect_kernel(offsets_ref, place_ref, other_ref, own_ref, *refs):
    early_refs, late_refs, out_ref, wide_refs = refs[:2], refs[2:4], refs[4], refs[5:]
    rows = own_ref.shape[0]

    @pl.when(pl.program_id(0) == 0)
    def _():
        is_first, is_last, seg = place_ref[FIRST] == 1, place_ref[LAST] == 1, place_ref[SEG]
        lowest, top = place_ref[LOWEST] == 1, place_ref[TOP] == 1
        width = own_ref.shape[1]
        unfold = lambda ref: jnp.concatenate([ref[...].astype(F32)[:DMAX], ref[...].astype(F32)[DMAX:]], axis=1)
        early, late = [unfold(ref) for ref in early_refs], [unfold(ref) for ref in late_refs]

        def widen(wide_ref, middle, lower, upper):
            lower = jnp.where(is_first, pltpu.roll(lower, 1, 1), lower)
            upper = jnp.where(is_last, pltpu.roll(upper, width - 1, 1), upper)
            for strip in range(width // LANES):
                at = slice(strip * LANES, (strip + 1) * LANES)
                wide_ref[strip, :DMAX] = lower[:, at]
                wide_ref[strip, DMAX : DMAX + rows] = middle[:, at]
                wide_ref[strip, DMAX + rows :] = upper[:, at]

        def place(own_wide, other_wide):
            lower = jnp.where(lowest, early[0], late[0]), jnp.where(lowest, late[0], early[0])
            upper = jnp.where(top, early[1], late[1]), jnp.where(top, late[1], early[1])
            widen(own_wide, own_ref[...], lower[0], upper[0])
            widen(other_wide, other_ref[...].astype(F32), lower[1], upper[1])

        @pl.when(seg == 0)
        def _():
            place(wide_refs[0], wide_refs[1])

        @pl.when(seg != 0)
        def _():
            place(wide_refs[1], wide_refs[0])

    for at in range(out_ref.shape[0]):
        template = pl.program_id(0) * out_ref.shape[0] + at
        begins = [DMAX + offsets_ref[template, s] for s in range(len(wide_refs))]
        for strip in range(own_ref.shape[1] // LANES):
            total = wide_refs[0][strip, pl.ds(begins[0], rows), :]
            for begin, wide_ref in zip(begins[1:], wide_refs[1:]):
                total = total + wide_ref[strip, pl.ds(begin, rows), :]
            out_ref[at, :, strip * LANES : (strip + 1) * LANES] = total * (1.0 / len(wide_refs))


def detect(offsets, place, other, own, early, late):
    templates = offsets.shape[0]
    rows, width = own.shape
    batch = 2 - templates % 2
    return pl.pallas_call(
        detect_kernel,
        grid=(templates // batch,),
        in_specs=[SMEM, SMEM] + [VMEM] * 6,
        out_specs=pl.BlockSpec((batch, rows, width), lambda t: (t, 0, 0)),
        out_shape=jax.ShapeDtypeStruct((templates, rows, width), F32),
        scratch_shapes=[pltpu.VMEM((width // LANES, rows + 2 * DMAX, LANES), F32)] * 2,
        compiler_params=params(8),
        cost_estimate=cost(3 * templates * rows * width, 4 * templates * rows * width),
        name="detect",
    )(offsets, place, other, own, *early, *late)


def local(series, antenna, offsets):
    devices = lax.axis_size("tm")
    index = lax.axis_index("tm")
    segs, _, rows, width = series.shape
    slow = devices * rows
    length = slow * width
    groups = devices // segs
    cols = width // groups
    seg, member = index // groups, index % groups
    place = jnp.stack([seg, member == 0, member == groups - 1, index == 0, index == devices - 1]).astype(jnp.int32)

    bins = np.arange(slow)
    short = [x.astype(BF16) for x in dft_table(bins, bins, slow)]
    fast = np.arange(width // 2)
    long = [x.astype(BF16) for parity in range(2) for x in dft_table(2 * fast + parity, fast, width)]
    order = np.concatenate([np.arange(0, cols, 2), np.arange(1, cols, 2)])
    bases = dft_table(bins, order, length)
    angle = (jnp.arange(slow, dtype=jnp.int32) * (member * cols) % length).astype(F32) * (2.0 * math.pi / length)
    turns = (jnp.cos(angle)[:, None], -jnp.sin(angle)[:, None])
    coef = lax.dynamic_index_in_dim(antenna, seg, 0, keepdims=False)
    scale = (coef[0] * coef[1] - coef[2] * coef[2]) * length
    coefs = coef * jnp.array([1.0, 1.0, 2.0], F32) / scale

    halves = [[g * groups + i for i in range(groups)] for g in range(segs)]
    trade = functools.partial(lax.all_to_all, axis_name="tm", split_axis=0, concat_axis=0, tiled=True)
    pieces = trade(pack(series, groups))

    turned = first_pass(pieces, order, short, bases, turns, groups)
    turned = trade(turned, axis_index_groups=halves)

    def move(x, by):
        return lax.ppermute(x, "tm", [(i, (i + by) % devices) for i in range(devices)])

    other, far_tail, far_head = fstat_pass(turned, 1 - seg[None], long, coefs, BF16)
    other = move(other, groups)
    own, tail, head = fstat_pass(turned, seg[None], long, coefs, F32)
    early = [move(far_tail, groups + 1), move(far_head, groups - 1)]
    late = [move(tail, 1), move(head, -1)]
    return detect(offsets, place, other, own, early, late)


def solution(mesh):
    return jax.shard_map(
        local,
        mesh=mesh,
        in_specs=(P("sky", None, "tm", None), P("sky", None), P("sky", None)),
        out_specs=P("sky", "tm", None),
        check_vma=False,
    )
```

time: 130 us -> 124 us (0.954)
  Pallas kernels: 31.8 us -> 26.8 us
  starting transfers between devices: 31.7 us -> 27.6 us
  waiting for transfers between devices: 58.6 us -> 61.1 us
    all_to_all x2 -> x1, waiting for transfers between devices: 9.62 us -> 22.5 us  [local(): turned = trade(turned, axis_index_groups=halves)]
    ppermute x5, waiting for transfers between devices: 11.8 us -> 1.44 us  [move(): lax.ppermute(x, 'tm', [(i, (i + by) % devices) for i in range(devices)])]
    pallas_call x5 -> x4, Pallas kernels: 29.2 us -> 24.2 us  [the longest x2 11.9 us: fstat_pass(): pl.pallas_call(fstat_kernel, grid_spec=pltpu.PrefetchScalarGridSpec(num_s...]
    all_to_all x2 -> x1, starting transfers between devices: 13.8 us -> 10.4 us  [local(): turned = trade(turned, axis_index_groups=halves)]
  transfers between devices with their start and end apart: 8 -> 7, of which waited for: 4 -> 3; matrix products, arithmetic and copies ran while one was open for 4% -> 4% of each run, Pallas kernels for 15% -> 5%
where the time goes in v1:
time: 124 us; the launch traced here: 123 us
  waiting for transfers between devices  61.1 us (49%)
  starting transfers between devices  27.6 us (22%)
  Pallas kernels  26.8 us (22%)
  other arithmetic  2.86 us (2%)
  between operations  2.63 us (2%)
  local copies, waits for them, and re-layouts  1.87 us (2%)
    all_to_all x1, waiting for transfers between devices, local(): pieces = trade(pack(series, groups))  37.2 us
    all_to_all x1, waiting for transfers between devices, local(): turned = trade(turned, axis_index_groups=halves)  22.5 us
    pallas_call x2, Pallas kernels, fstat_pass(): pl.pallas_call(fstat_kernel, grid_spec=pltpu.PrefetchScalarGridSpec(num_s...  11.9 us
    all_to_all x1, starting transfers between devices, local(): turned = trade(turned, axis_index_groups=halves)  10.4 us
    ppermute x5, starting transfers between devices, move(): lax.ppermute(x, 'tm', [(i, (i + by) % devices) for i in range(devices)])  9.83 us
    pallas_call x1, Pallas kernels, first_pass(): pl.pallas_call(first_kernel, grid=(segs * steps,), in_specs=[pl.BlockSpec...  8.85 us
    all_to_all x1, starting transfers between devices, local(): pieces = trade(pack(series, groups))  7.39 us
    pallas_call x1, Pallas kernels, detect(): pl.pallas_call(detect_kernel, grid=(templates // batch,), in_specs=[SMEM,...  3.43 us
  transfers between devices with their start and end apart: 7, of which 3 were waited for; matrix products, arithmetic and copies ran while one was open for 4% of the time, Pallas kernels for 5%

profile of v1, /device:TPU:0, one launch (start us, length us, event | category | flops | bytes accessed | tf_op | source)
XLA Modules:
  0.0 122.9 jit_solution(14851745842279849671)
XLA Ops:
  0.0 2.6 %pack.1 = bf16[16,4,64,256]{3,2,1,0:T(8,128)(2,1)} custom-call(bf16[2,4,64,2048]{3,2,1,0:T(8,128)(2,1)} %x_ref.1), custom_call_target="tpu_custom_call" | custom-call | bytes 4194304 | tf_op jit(solution)/shard_map/pack/pallas_call | solution.py:53
  2.6 7.4 %all-to-all-start = ((bf16[16,4,64,256]{3,2,1,0:T(8,128)(2,1)}), bf16[16,4,64,256]{3,2,1,0:T(8,128)(2,1)S(1)}, u32[]{:S(2)}, u32[]{:S(2)}) async-start(bf16[16,4,64,256]{3,2,1,0:T(8,128)(2,1)} %pack.1), calls=%async_computation | async-start | bytes 4194304 | tf_op jit(solution)/shard_map/all_to_all | solution.py:265
  10.1 1.0 copy.15
  11.1 2.8 %sine_negate_fusion = (f32[1024,1]{1,0:T(8,128)S(1)}, f32[1024,1]{1,0:T(8,128)S(1)}) fusion(f32[1024,1]{1,0:T(8,128)} %copy.15), kind=kLoop, calls=%fused_computation | loop fusion | flops 2048 | bytes 12288 | tf_op jit(solution)/shard_map/neg | solution.py:258
  13.9 37.2 %all-to-all-done.x_ref = bf16[16,4,64,256]{3,2,1,0:T(8,128)(2,1)S(1)} async-done(((bf16[16,4,64,256]{3,2,1,0:T(8,128)(2,1)}), bf16[16,4,64,256]{3,2,1,0:T(8,128)(2,1)S(1)}, u32[]{:S(2)}, u32[]{:S(2)}) %all-to-all-start) | async-done | bytes 2097184 | tf_op jit(solution)/shard_map/all_to_all | solution.py:265
  51.1 8.9 %first_pass.1 = bf16[8,2,4,64,256]{4,3,2,1,0:T(8,128)(2,1)} custom-call(bf16[16,4,64,256]{3,2,1,0:T(8,128)(2,1)S(1)} %all-to-all-done.x_ref, bf16[256,256]{1,0:T(8,128)(2,1)} %constant.79.clone.sort_ref, bf16[1024,1024]{1,0:T(8,128)(2,1)} %constant.80.clone.wr_ref.er_ref, bf16[1024,1024]{1,0:T(8,128)(2,1)} %constant.81.clone.wi_ref.ei_ref, ...), custom_call_target="tpu_custom_call" | custom-call | flops 4294967296 | bytes 4194304 | tf_op jit(solution)/shard_map/first_pass/pallas_call | solution.py:95
  60.0 0.0 copy-start.2
  60.0 0.0 copy-start.1
  60.0 10.4 %all-to-all-start.1 = ((bf16[8,2,4,64,256]{4,3,2,1,0:T(8,128)(2,1)}), bf16[8,2,4,64,256]{4,3,2,1,0:T(8,128)(2,1)S(1)}, u32[]{:S(2)}, u32[]{:S(2)}) async-start(bf16[8,2,4,64,256]{4,3,2,1,0:T(8,128)(2,1)} %first_pass.1), calls=%async_computation.1 | async-start | bytes 4194304 | tf_op jit(solution)/shard_map/all_to_all | solution.py:268
  70.4 0.0 copy-done.2
  70.4 0.7 fusion.2
  73.6 0.0 copy-done.1
  73.6 22.5 %all-to-all-done.1.z_ref = bf16[8,2,4,64,256]{4,3,2,1,0:T(8,128)(2,1)S(1)} async-done(((bf16[8,2,4,64,256]{4,3,2,1,0:T(8,128)(2,1)}), bf16[8,2,4,64,256]{4,3,2,1,0:T(8,128)(2,1)S(1)}, u32[]{:S(2)}, u32[]{:S(2)}) %all-to-all-start.1) | async-done | bytes 2097184 | tf_op jit(solution)/shard_map/all_to_all | solution.py:268
  96.1 6.0 %fstat_pass.2 = (bf16[64,2048]{1,0:T(8,128)(2,1)S(1)}, bf16[16,1024]{1,0:T(8,128)(2,1)S(1)}, bf16[16,1024]{1,0:T(8,128)(2,1)S(1)}) custom-call(s32[1]{0:T(128)S(6)} %sub.12.half_ref, f32[3]{0:T(128)S(1)} %divide_bitcast_fusion.coef_ref, bf16[8,2,4,64,256]{4,3,2,1,0:T(8,128)(2,1)S(1)} %all-to-all-done.1.z_ref, ...), custom_call_target="tpu_custom_call" | custom-call | flops 2147483648 | bytes 8388608 | tf_op jit(solution)/shard_map/fstat_pass/pallas_call | solution.py:161
  102.1 0.0 copy-start
  102.1 2.7 %collective-permute-start = (bf16[64,2048]{1,0:T(8,128)(2,1)S(1)}, bf16[64,2048]{1,0:T(8,128)(2,1)S(1)}, u32[]{:S(2)}, u32[]{:S(2)}) collective-permute-start(bf16[64,2048]{1,0:T(8,128)(2,1)S(1)} %get-tuple-element.11), channel_id=1, source_target_pairs={{0,8},{1,9},{2,10},{3,11},{4,12},{5,13},{6,14},{7,15},{8,0},{9,1},... | collective-permute-start | bytes 786440 | tf_op jit(solution)/shard_map/ppermute | solution.py:271
  104.8 6.0 %fstat_pass.3 = (f32[64,2048]{1,0:T(8,128)S(1)}, f32[16,1024]{1,0:T(8,128)S(1)}, f32[16,1024]{1,0:T(8,128)S(1)}) custom-call(s32[1]{0:T(128)} %bitcast.half_ref, f32[3]{0:T(128)S(1)} %divide_bitcast_fusion.coef_ref, bf16[8,2,4,64,256]{4,3,2,1,0:T(8,128)(2,1)S(1)} %all-to-all-done.1.z_ref, bf16[1024,1024]{1,0:T(8,128)(2,1)} %constant.80.clone.wr_ref.er_ref, ...), custom_call_target="tpu_custom_call" | custom-call | flops 2147483648 | bytes 8388608 | tf_op jit(solution)/shard_map/fstat_pass/pallas_call | solution.py:161
  110.8 0.1 collective-permute-start.3
  110.8 4.4 %collective-permute-start.4 = (f32[16,1024]{1,0:T(8,128)S(1)}, f32[16,1024]{1,0:T(8,128)S(1)}, u32[]{:S(2)}, u32[]{:S(2)}) collective-permute-start(f32[16,1024]{1,0:T(8,128)S(1)} %get-tuple-element.16), channel_id=1, source_target_pairs={{0,15},{1,0},{2,1},{3,2},{4,3},{5,4},{6,5},{7,6},{8,7},{9,8},{10,9... | collective-permute-start | bytes 196616 | tf_op jit(solution)/shard_map/ppermute | solution.py:271
  115.3 0.0 collective-permute-start.1
  115.3 2.6 %collective-permute-start.2 = (bf16[16,1024]{1,0:T(8,128)(2,1)S(1)}, bf16[16,1024]{1,0:T(8,128)(2,1)S(1)}, u32[]{:S(2)}, u32[]{:S(2)}) collective-permute-start(bf16[16,1024]{1,0:T(8,128)(2,1)S(1)} %get-tuple-element.14), channel_id=1, source_target_pairs={{0,7},{1,8},{2,9},{3,10},{4,11},{5,12},{6,13},{7,14},{8,15},{9,0},... | collective-permute-start | bytes 98312 | tf_op jit(solution)/shard_map/ppermute | solution.py:271
  117.9 0.0 copy-done
  117.9 0.1 copy.16.offsets_ref
  118.0 0.1 stack.39.place_ref
  118.1 1.4 %collective-permute-done.1.refs_0_ = bf16[16,1024]{1,0:T(8,128)(2,1)S(1)} collective-permute-done((bf16[16,1024]{1,0:T(8,128)(2,1)S(1)}, bf16[16,1024]{1,0:T(8,128)(2,1)S(1)}, u32[]{:S(2)}, u32[]{:S(2)}) %collective-permute-start.1) | collective-permute-done | bytes 32800 | tf_op jit(solution)/shard_map/ppermute | solution.py:271
  119.5 0.0 collective-permute-done.2.refs_1_
  119.5 0.0 collective-permute-done.3.refs_2_
  119.5 0.0 collective-permute-done.4.refs_3_
  119.5 0.0 collective-permute-done.other_ref
  119.5 3.4 %detect.1 = f32[8,64,2048]{2,1,0:T(8,128)} custom-call(s32[8,2]{1,0:T(8,128)S(1)} %copy.16.offsets_ref, s32[5]{0:T(128)S(1)} %stack.39.place_ref, bf16[64,2048]{1,0:T(8,128)(2,1)S(1)} %collective-permute-done.other_ref, f32[64,2048]{1,0:T(8,128)S(1)} %get-tuple-element.12.own_ref, bf16[16,1024]{1,0:T(8,128)(2,1)S(1)} %collective-permute-done.1.refs_0_, ...), custom_call_target="tpu_custom_call" | custom-call | flops 3145728 | bytes 4194304 | tf_op jit(solution)/shard_map/detect/pallas_call | solution.py:227
  (3 shorter events, 0.0 us)
Async XLA Ops:
  2.6 48.5 %all-to-all-start = ((bf16[16,4,64,256]{3,2,1,0:T(8,128)(2,1)}), bf16[16,4,64,256]{3,2,1,0:T(8,128)(2,1)S(1)}, u32[]{:S(2)}, u32[]{:S(2)}) async-start(bf16[16,4,64,256]{3,2,1,0:T(8,128)(2,1)} %pack.1), calls=%async_computation | async-start | bytes 4194304 | tf_op jit(solution)/shard_map/all_to_all | solution.py:265
  60.0 10.4 %copy-start.2 = (f32[2,3]{1,0:T(2,128)S(1)}, f32[2,3]{1,0:T(2,128)}, u32[]{:S(2)}) copy-start(f32[2,3]{1,0:T(2,128)} %param.14) | copy-start | bytes 76
  60.0 13.6 %copy-start.1 = (f32[1,3]{1,0:T(1,128)S(1)}, f32[1,3]{1,0:T(1,128)}, u32[]{:S(2)}) copy-start(f32[1,3]{1,0:T(1,128)} %constant.86) | copy-start | bytes 40
  60.0 36.1 %all-to-all-start.1 = ((bf16[8,2,4,64,256]{4,3,2,1,0:T(8,128)(2,1)}), bf16[8,2,4,64,256]{4,3,2,1,0:T(8,128)(2,1)S(1)}, u32[]{:S(2)}, u32[]{:S(2)}) async-start(bf16[8,2,4,64,256]{4,3,2,1,0:T(8,128)(2,1)} %first_pass.1), calls=%async_computation.1 | async-start | bytes 4194304 | tf_op jit(solution)/shard_map/all_to_all | solution.py:268
  102.1 15.8 %copy-start = (s32[8,2]{0,1:T(2,128)S(1)}, s32[8,2]{0,1:T(2,128)}, u32[]{:S(2)}) copy-start(s32[8,2]{0,1:T(2,128)} %param.15) | copy-start | bytes 196
  102.1 17.4 %collective-permute-start = (bf16[64,2048]{1,0:T(8,128)(2,1)S(1)}, bf16[64,2048]{1,0:T(8,128)(2,1)S(1)}, u32[]{:S(2)}, u32[]{:S(2)}) collective-permute-start(bf16[64,2048]{1,0:T(8,128)(2,1)S(1)} %get-tuple-element.11), channel_id=1, source_target_pairs={{0,8},{1,9},{2,10},{3,11},{4,12},{5,13},{6,14},{7,15},{8,0},{9,1},... | collective-permute-start | bytes 786440 | tf_op jit(solution)/shard_map/ppermute | solution.py:271
  110.8 8.7 %collective-permute-start.3 = (f32[16,1024]{1,0:T(8,128)S(1)}, f32[16,1024]{1,0:T(8,128)S(1)}, u32[]{:S(2)}, u32[]{:S(2)}) collective-permute-start(f32[16,1024]{1,0:T(8,128)S(1)} %get-tuple-element.15), channel_id=1, source_target_pairs={{0,1},{1,2},{2,3},{3,4},{4,5},{5,6},{6,7},{7,8},{8,9},{9,10},{10,1... | collective-permute-start | bytes 196616 | tf_op jit(solution)/shard_map/ppermute | solution.py:271
  110.8 8.7 %collective-permute-start.4 = (f32[16,1024]{1,0:T(8,128)S(1)}, f32[16,1024]{1,0:T(8,128)S(1)}, u32[]{:S(2)}, u32[]{:S(2)}) collective-permute-start(f32[16,1024]{1,0:T(8,128)S(1)} %get-tuple-element.16), channel_id=1, source_target_pairs={{0,15},{1,0},{2,1},{3,2},{4,3},{5,4},{6,5},{7,6},{8,7},{9,8},{10,9... | collective-permute-start | bytes 196616 | tf_op jit(solution)/shard_map/ppermute | solution.py:271
  115.3 4.2 %collective-permute-start.1 = (bf16[16,1024]{1,0:T(8,128)(2,1)S(1)}, bf16[16,1024]{1,0:T(8,128)(2,1)S(1)}, u32[]{:S(2)}, u32[]{:S(2)}) collective-permute-start(bf16[16,1024]{1,0:T(8,128)(2,1)S(1)} %get-tuple-element.13), channel_id=1, source_target_pairs={{0,9},{1,10},{2,11},{3,12},{4,13},{5,14},{6,15},{7,0},{8,1},{9,2},... | collective-permute-start | bytes 98312 | tf_op jit(solution)/shard_map/ppermute | solution.py:271
  115.3 4.2 %collective-permute-start.2 = (bf16[16,1024]{1,0:T(8,128)(2,1)S(1)}, bf16[16,1024]{1,0:T(8,128)(2,1)S(1)}, u32[]{:S(2)}, u32[]{:S(2)}) collective-permute-start(bf16[16,1024]{1,0:T(8,128)(2,1)S(1)} %get-tuple-element.14), channel_id=1, source_target_pairs={{0,7},{1,8},{2,9},{3,10},{4,11},{5,12},{6,13},{7,14},{8,15},{9,0},... | collective-permute-start | bytes 98312 | tf_op jit(solution)/shard_map/ppermute | solution.py:271

commit v2 on v1

--- a/solution.py
+++ b/solution.py
@@ -41,84 +41,84 @@
     return jnp.dot(x, y, preferred_element_type=F32)
 
 
-def pack_kernel(x_ref, out_ref):
-    cols = out_ref.shape[-1]
+def pack_kernel(x_ref, sort_ref, out_ref):
+    _, comps, rows, cols = out_ref.shape
     for piece in range(out_ref.shape[0]):
-        out_ref[piece] = x_ref[0, :, :, piece * cols : (piece + 1) * cols]
-
-
-def pack(series, groups):
+        x = x_ref[0, :, :, piece * cols : (piece + 1) * cols].reshape(comps * rows, cols)
+        out_ref[piece] = dot(x, sort_ref[...]).astype(BF16).reshape(comps, rows, cols)
+
+
+def pack(series, order, groups):
     segs, comps, rows, width = series.shape
-    shape = (segs * groups, comps, rows, width // groups)
+    cols = width // groups
+    batch = max(1, groups // 2)
+    shape = (segs * groups, comps, rows, cols)
+    sort = np.zeros((cols, cols), np.float32)
+    sort[order, np.arange(cols)] = 1.0
     return pl.pallas_call(
         pack_kernel,
-        grid=(segs,),
-        in_specs=[pl.BlockSpec((1, comps, rows, width), lambda s: (s, 0, 0, 0))],
-        out_specs=pl.BlockSpec((groups,) + shape[1:], lambda s: (s, 0, 0, 0)),
+        grid=(segs, groups // batch),
+        in_specs=[
+            pl.BlockSpec((1, comps, rows, batch * cols), lambda s, t: (s, 0, 0, t)),
+            pl.BlockSpec((cols, cols), lambda s, t: (0, 0)),
+        ],
+        out_specs=pl.BlockSpec((batch,) + shape[1:], lambda s, t: (s * (groups // batch) + t, 0, 0, 0)),
         out_shape=pltpu.HBM(shape, BF16),
         compiler_params=params(16),
-        cost_estimate=cost(0, 4 * math.prod(shape)),
+        cost_estimate=cost(2 * math.prod(shape) * cols, 4 * math.prod(shape)),
         name="pack",
-    )(in_hbm(series))
-
-
-def first_kernel(x_ref, sort_ref, wr_ref, wi_ref, br_ref, bi_ref, vr_ref, vi_ref, out_ref, sorted_ref):
+    )(in_hbm(series), in_hbm(sort.astype(BF16)))
+
+
+def first_kernel(half_ref, x_ref, wr_ref, wi_ref, br_ref, bi_ref, vr_ref, vi_ref, out_ref):
     length = wr_ref.shape[1]
-    comps, cols = x_ref.shape[1], x_ref.shape[-1]
-
-    @pl.when(pl.program_id(0) == 0)
-    def _():
-        for comp in range(comps):
-            sorted_ref[comp] = dot(x_ref[:, comp].reshape(length, cols), sort_ref[...]).astype(BF16)
-
-    shape = (out_ref.shape[0],) + out_ref.shape[3:]
+    cols = x_ref.shape[-1]
+    shape = (out_ref.shape[0],) + out_ref.shape[2:]
     by_real, by_imag = vr_ref[...], vi_ref[...]
     t_real = br_ref[...] * by_real - bi_ref[...] * by_imag
     t_imag = br_ref[...] * by_imag + bi_ref[...] * by_real
-    for lead in range(0, comps, 2):
-        x_real, x_imag = sorted_ref[lead], sorted_ref[lead + 1]
+    for lead in range(0, x_ref.shape[1], 2):
+        x_real = x_ref[:, lead].reshape(length, cols)
+        x_imag = x_ref[:, lead + 1].reshape(length, cols)
         real_part = dot(wr_ref[...], x_real) - dot(wi_ref[...], x_imag)
         imag_part = dot(wi_ref[...], x_real) + dot(wr_ref[...], x_imag)
-        out_ref[:, 0, lead] = (real_part * t_real - imag_part * t_imag).astype(BF16).reshape(shape)
-        out_ref[:, 0, lead + 1] = (real_part * t_imag + imag_part * t_real).astype(BF16).reshape(shape)
-
-
-def first_pass(pieces, order, tables, bases, turns, groups):
+        out_ref[:, lead] = (real_part * t_real - imag_part * t_imag).astype(BF16).reshape(shape)
+        out_ref[:, lead + 1] = (real_part * t_imag + imag_part * t_real).astype(BF16).reshape(shape)
+
+
+def first_pass(pieces, half, tables, bases, turns, groups):
     count, comps, rows, cols = pieces.shape
     length = count * rows
-    segs = count // groups
-    tile = min(256, groups * rows)
-    steps = groups * rows // tile
-    sort = np.zeros((cols, cols), np.float32)
-    sort[order, np.arange(cols)] = 1.0
-    strip = lambda width: pl.BlockSpec((tile, width), lambda t: (t, 0))
+    per_half = groups * rows
+    tile = min(256, per_half)
+    steps = per_half // tile
+    strip = lambda width: pl.BlockSpec((tile, width), lambda t, half: (half[0] * steps + t, 0))
     return pl.pallas_call(
         first_kernel,
-        grid=(segs * steps,),
-        in_specs=[
-            pl.BlockSpec(pieces.shape, lambda t: (0, 0, 0, 0)),
-            pl.BlockSpec((cols, cols), lambda t: (0, 0)),
-        ]
-        + [strip(length)] * 2
-        + [strip(cols)] * 2
-        + [strip(1)] * 2,
-        out_specs=pl.BlockSpec((tile // rows, 1, comps, rows, cols), lambda t: (t % steps, t // steps, 0, 0, 0)),
-        out_shape=pltpu.HBM((groups, segs, comps, rows, cols), BF16),
-        scratch_shapes=[pltpu.VMEM((comps, length, cols), BF16)],
+        grid_spec=pltpu.PrefetchScalarGridSpec(
+            num_scalar_prefetch=1,
+            grid=(steps,),
+            in_specs=[pl.BlockSpec(pieces.shape, lambda t, half: (0, 0, 0, 0))]
+            + [strip(length)] * 2
+            + [strip(cols)] * 2
+            + [strip(1)] * 2,
+            out_specs=pl.BlockSpec((tile // rows, comps, rows, cols), lambda t, half: (t, 0, 0, 0)),
+        ),
+        out_shape=pltpu.HBM((groups, comps, rows, cols), BF16),
         compiler_params=params(24),
-        cost_estimate=cost(4 * comps * length * length * cols, 4 * length * length),
+        cost_estimate=cost(4 * comps * per_half * length * cols, 4 * per_half * length),
         name="first_pass",
-    )(pieces, in_hbm(sort.astype(BF16)), *map(in_hbm, tables), *map(in_hbm, bases), *turns)
-
-
-def fstat_kernel(half_ref, coef_ref, z_ref, er_ref, ei_ref, or_ref, oi_ref, fstat_ref, tail_ref, head_ref, lhs_ref):
+    )(half, pieces, *map(in_hbm, tables), *map(in_hbm, bases), *turns)
+
+
+def fstat_kernel(coef_ref, z_ref, er_ref, ei_ref, or_ref, oi_ref, fstat_ref, tail_ref, head_ref, lhs_ref):
     step = pl.program_id(0)
 
     @pl.when(step == 0)
     def _():
         groups, cols = z_ref.shape[0], z_ref.shape[-1] // 2
         for source in range(groups):
-            piece = z_ref[source, 0].reshape(lhs_ref.shape[1], 2 * cols)
+            piece = z_ref[source].reshape(lhs_ref.shape[1], 2 * cols)
             for parity in range(2):
                 at = slice(source * cols, (source + 1) * cols)
                 lhs_ref[parity, :, at] = piece[:, parity * cols : (parity + 1) * cols]
@@ -151,28 +151,24 @@
     head_ref[:, at] = jnp.concatenate(heads, axis=0).astype(head_ref.dtype)
 
 
-def fstat_pass(z, half, tables, coefs, kind):
-    groups, _, comps, rows, cols = z.shape
+def fstat_pass(z, tables, coefs, kind):
+    groups, comps, rows, cols = z.shape
     width = groups * cols
     span = width // 2
     tile = min(256, span)
     rim = (2 * DMAX, span)
-    still = lambda shape: pl.BlockSpec(shape, lambda t, half: (0,) * len(shape))
+    still = lambda shape: pl.BlockSpec(shape, lambda t: (0,) * len(shape))
     return pl.pallas_call(
         fstat_kernel,
-        grid_spec=pltpu.PrefetchScalarGridSpec(
-            num_scalar_prefetch=1,
-            grid=(span // tile,),
-            in_specs=[SMEM, pl.BlockSpec((groups, 1, comps, rows, cols), lambda t, half: (0, half[0], 0, 0, 0))]
-            + [pl.BlockSpec((span, tile), lambda t, half: (0, t))] * 4,
-            out_specs=[still((rows, width)), still(rim), still(rim)],
-            scratch_shapes=[pltpu.VMEM((2, comps * rows, span), BF16)],
-        ),
+        grid=(span // tile,),
+        in_specs=[SMEM, still(z.shape)] + [pl.BlockSpec((span, tile), lambda t: (0, t))] * 4,
+        out_specs=[still((rows, width)), still(rim), still(rim)],
         out_shape=[jax.ShapeDtypeStruct((rows, width), kind)] + [jax.ShapeDtypeStruct(rim, kind)] * 2,
+        scratch_shapes=[pltpu.VMEM((2, comps * rows, span), BF16)],
         compiler_params=params(24),
         cost_estimate=cost(2 * comps * rows * width * width, 2 * width * width),
         name="fstat_pass",
-    )(half, coefs, z, *map(in_hbm, tables))
+    )(coefs, z, *map(in_hbm, tables))
 
 
 def detect_kernel(offsets_ref, place_ref, other_ref, own_ref, *refs):
@@ -262,17 +258,19 @@
 
     halves = [[g * groups + i for i in range(groups)] for g in range(segs)]
     trade = functools.partial(lax.all_to_all, axis_name="tm", split_axis=0, concat_axis=0, tiled=True)
-    pieces = trade(pack(series, groups))
-
-    turned = first_pass(pieces, order, short, bases, turns, groups)
-    turned = trade(turned, axis_index_groups=halves)
+    pieces = trade(pack(series, order, groups))
+
+    def rows_of(half):
+        turned = first_pass(pieces, half[None], short, bases, turns, groups)
+        return trade(turned, axis_index_groups=halves)
 
     def move(x, by):
         return lax.ppermute(x, "tm", [(i, (i + by) % devices) for i in range(devices)])
 
-    other, far_tail, far_head = fstat_pass(turned, 1 - seg[None], long, coefs, BF16)
+    far, near = rows_of(1 - seg), rows_of(seg)
+    other, far_tail, far_head = fstat_pass(far, long, coefs, BF16)
     other = move(other, groups)
-    own, tail, head = fstat_pass(turned, seg[None], long, coefs, F32)
+    own, tail, head = fstat_pass(near, long, coefs, F32)
     early = [move(far_tail, groups + 1), move(far_head, groups - 1)]
     late = [move(tail, 1), move(head, -1)]
     return detect(offsets, place, other, own, early, late)

time: 124 us -> 122 us (0.984)
  waiting for transfers between devices: 61.1 us -> 50.8 us
  starting transfers between devices: 27.6 us -> 31.6 us
  Pallas kernels: 26.8 us -> 30 us
    all_to_all x2 -> x3, waiting for transfers between devices: 59.7 us -> 48.2 us  [the longest x1 37.2 us: local(): pieces = trade(pack(series, order, groups))]
    all_to_all x2 -> x3, starting transfers between devices: 17.8 us -> 21.2 us  [the longest x2 13.8 us: rows_of(): return trade(turned, axis_index_groups=halves)]
    pallas_call x4 -> x5, Pallas kernels: 23.4 us -> 26.6 us  [the longest x2 12.4 us: fstat_pass(): pl.pallas_call(fstat_kernel, grid=(span // tile,), in_specs=[SMEM, still(...]
  transfers between devices with their start and end apart: 7 -> 8, of which waited for: 3 -> 5; matrix products, arithmetic and copies ran while one was open for 4% -> 4% of each run, Pallas kernels for 5% -> 14%
where the time goes in v2:
time: 122 us; the launch traced here: 120 us
  waiting for transfers between devices  50.8 us (42%)
  starting transfers between devices  31.6 us (26%)
  Pallas kernels  30 us (25%)
  other arithmetic  2.86 us (2%)
  between operations  2.67 us (2%)
  local copies, waits for them, and re-layouts  1.87 us (2%)
    all_to_all x1, waiting for transfers between devices, local(): pieces = trade(pack(series, order, groups))  37.2 us
    all_to_all x2, starting transfers between devices, rows_of(): return trade(turned, axis_index_groups=halves)  13.8 us
    pallas_call x2, Pallas kernels, fstat_pass(): pl.pallas_call(fstat_kernel, grid=(span // tile,), in_specs=[SMEM, still(...  12.4 us
    all_to_all x2, waiting for transfers between devices, rows_of(): return trade(turned, axis_index_groups=halves)  11 us
    ppermute x5, starting transfers between devices, move(): lax.ppermute(x, 'tm', [(i, (i + by) % devices) for i in range(devices)])  10.4 us
    pallas_call x2, Pallas kernels, first_pass(): pl.pallas_call(first_kernel, grid_spec=pltpu.PrefetchScalarGridSpec(num_s...  9.82 us
    all_to_all x1, starting transfers between devices, local(): pieces = trade(pack(series, order, groups))  7.38 us
    pallas_call x1, Pallas kernels, pack(): pl.pallas_call(pack_kernel, grid=(segs, groups // batch), in_specs=[pl.Bl...  4.33 us
  transfers between devices with their start and end apart: 8, of which 5 were waited for; matrix products, arithmetic and copies ran while one was open for 4% of the time, Pallas kernels for 14%

profile of v2, /device:TPU:0, one launch (start us, length us, event | category | flops | bytes accessed | tf_op | source)
XLA Modules:
  0.0 119.9 jit_solution(16315364610121309258)
XLA Ops:
  0.0 4.3 %pack.1 = bf16[16,4,64,256]{3,2,1,0:T(8,128)(2,1)} custom-call(bf16[2,4,64,2048]{3,2,1,0:T(8,128)(2,1)} %x_ref.1, bf16[256,256]{1,0:T(8,128)(2,1)} %constant.78.clone.sort_ref), custom_call_target="tpu_custom_call" | custom-call | flops 536870912 | bytes 4194304 | tf_op jit(solution)/shard_map/pack/pallas_call | solution.py:58
  4.3 7.4 %all-to-all-start = ((bf16[16,4,64,256]{3,2,1,0:T(8,128)(2,1)}), bf16[16,4,64,256]{3,2,1,0:T(8,128)(2,1)S(1)}, u32[]{:S(2)}, u32[]{:S(2)}) async-start(bf16[16,4,64,256]{3,2,1,0:T(8,128)(2,1)} %pack.1), calls=%async_computation | async-start | bytes 4194304 | tf_op jit(solution)/shard_map/all_to_all | solution.py:261
  11.8 1.0 copy.15
  12.8 2.8 %sine_negate_fusion = (f32[1024,1]{1,0:T(8,128)S(1)}, f32[1024,1]{1,0:T(8,128)S(1)}) fusion(f32[1024,1]{1,0:T(8,128)} %copy.15), kind=kLoop, calls=%fused_computation | loop fusion | flops 2048 | bytes 12288 | tf_op jit(solution)/shard_map/neg | solution.py:254
  15.6 37.2 %all-to-all-done.x_ref = bf16[16,4,64,256]{3,2,1,0:T(8,128)(2,1)S(1)} async-done(((bf16[16,4,64,256]{3,2,1,0:T(8,128)(2,1)}), bf16[16,4,64,256]{3,2,1,0:T(8,128)(2,1)S(1)}, u32[]{:S(2)}, u32[]{:S(2)}) %all-to-all-start) | async-done | bytes 2097184 | tf_op jit(solution)/shard_map/all_to_all | solution.py:261
  52.8 4.9 %first_pass.2 = bf16[8,4,64,256]{3,2,1,0:T(8,128)(2,1)} custom-call(s32[1]{0:T(128)} %bitcast.7.half_ref, bf16[16,4,64,256]{3,2,1,0:T(8,128)(2,1)S(1)} %all-to-all-done.x_ref, bf16[1024,1024]{1,0:T(8,128)(2,1)} %constant.79.clone.wr_ref.er_ref, bf16[1024,1024]{1,0:T(8,128)(2,1)} %constant.80.clone.wi_ref.ei_ref, f32[1024,256]{1,0:T(8,128)} %constant.81.clone.br_ref, ...), custom_call_target="tpu_custom_call" | custom-call | flops 2147483648 | bytes 2097152 | tf_op jit(solution)/shard_map/first_pass/pallas_call | solution.py:96
  57.7 10.3 %all-to-all-start.1 = ((bf16[8,4,64,256]{3,2,1,0:T(8,128)(2,1)}), bf16[8,4,64,256]{3,2,1,0:T(8,128)(2,1)}, u32[]{:S(2)}, u32[]{:S(2)}) async-start(bf16[8,4,64,256]{3,2,1,0:T(8,128)(2,1)} %first_pass.2), calls=%async_computation.1 | async-start | bytes 2097152 | tf_op jit(solution)/shard_map/all_to_all | solution.py:265
  68.0 4.9 %first_pass.3 = bf16[8,4,64,256]{3,2,1,0:T(8,128)(2,1)} custom-call(s32[1]{0:T(128)} %bitcast.half_ref, bf16[16,4,64,256]{3,2,1,0:T(8,128)(2,1)S(1)} %all-to-all-done.x_ref, bf16[1024,1024]{1,0:T(8,128)(2,1)} %constant.79.clone.wr_ref.er_ref, bf16[1024,1024]{1,0:T(8,128)(2,1)} %constant.80.clone.wi_ref.ei_ref, f32[1024,256]{1,0:T(8,128)} %constant.81.clone.br_ref, ...), custom_call_target="tpu_custom_call" | custom-call | flops 2147483648 | bytes 2097152 | tf_op jit(solution)/shard_map/first_pass/pallas_call | solution.py:96
  72.9 0.0 copy-start.2
  72.9 9.6 %all-to-all-done.1.z_ref = bf16[8,4,64,256]{3,2,1,0:T(8,128)(2,1)} async-done(((bf16[8,4,64,256]{3,2,1,0:T(8,128)(2,1)}), bf16[8,4,64,256]{3,2,1,0:T(8,128)(2,1)}, u32[]{:S(2)}, u32[]{:S(2)}) %all-to-all-start.1) | async-done | bytes 1048608 | tf_op jit(solution)/shard_map/all_to_all | solution.py:265
  82.6 3.6 %all-to-all-start.2 = ((bf16[8,4,64,256]{3,2,1,0:T(8,128)(2,1)}), bf16[8,4,64,256]{3,2,1,0:T(8,128)(2,1)S(1)}, u32[]{:S(2)}, u32[]{:S(2)}) async-start(bf16[8,4,64,256]{3,2,1,0:T(8,128)(2,1)} %first_pass.3), calls=%async_computation.2 | async-start | bytes 2097152 | tf_op jit(solution)/shard_map/all_to_all | solution.py:265
  86.1 0.0 copy-done.2
  86.2 0.7 fusion.2
  89.3 0.0 copy-done.1
  89.4 6.5 %fstat_pass.2 = (bf16[64,2048]{1,0:T(8,128)(2,1)S(1)}, bf16[16,1024]{1,0:T(8,128)(2,1)S(1)}, bf16[16,1024]{1,0:T(8,128)(2,1)S(1)}) custom-call(f32[3]{0:T(128)S(1)} %divide_bitcast_fusion.coef_ref, bf16[8,4,64,256]{3,2,1,0:T(8,128)(2,1)} %all-to-all-done.1.z_ref, bf16[1024,1024]{1,0:T(8,128)(2,1)} %constant.79.clone.wr_ref.er_ref, ...), custom_call_target="tpu_custom_call" | custom-call | flops 2147483648 | bytes 8388608 | tf_op jit(solution)/shard_map/fstat_pass/pallas_call | solution.py:161
  95.9 0.0 copy-start
  95.9 3.3 %collective-permute-start = (bf16[64,2048]{1,0:T(8,128)(2,1)S(1)}, bf16[64,2048]{1,0:T(8,128)(2,1)S(1)}, u32[]{:S(2)}, u32[]{:S(2)}) collective-permute-start(bf16[64,2048]{1,0:T(8,128)(2,1)S(1)} %get-tuple-element.11), channel_id=1, source_target_pairs={{0,8},{1,9},{2,10},{3,11},{4,12},{5,13},{6,14},{7,15},{8,0},{9,1},... | collective-permute-start | bytes 786440 | tf_op jit(solution)/shard_map/ppermute | solution.py:268
  99.2 1.3 %all-to-all-done.2.z_ref = bf16[8,4,64,256]{3,2,1,0:T(8,128)(2,1)S(1)} async-done(((bf16[8,4,64,256]{3,2,1,0:T(8,128)(2,1)}), bf16[8,4,64,256]{3,2,1,0:T(8,128)(2,1)S(1)}, u32[]{:S(2)}, u32[]{:S(2)}) %all-to-all-start.2) | async-done | bytes 1048608 | tf_op jit(solution)/shard_map/all_to_all | solution.py:265
  100.5 6.0 %fstat_pass.3 = (f32[64,2048]{1,0:T(8,128)S(1)}, f32[16,1024]{1,0:T(8,128)S(1)}, f32[16,1024]{1,0:T(8,128)S(1)}) custom-call(f32[3]{0:T(128)S(1)} %divide_bitcast_fusion.coef_ref, bf16[8,4,64,256]{3,2,1,0:T(8,128)(2,1)S(1)} %all-to-all-done.2.z_ref, bf16[1024,1024]{1,0:T(8,128)(2,1)} %constant.79.clone.wr_ref.er_ref, ...), custom_call_target="tpu_custom_call" | custom-call | flops 2147483648 | bytes 8388608 | tf_op jit(solution)/shard_map/fstat_pass/pallas_call | solution.py:161
  106.5 0.1 collective-permute-start.3
  106.5 4.4 %collective-permute-start.4 = (f32[16,1024]{1,0:T(8,128)S(1)}, f32[16,1024]{1,0:T(8,128)S(1)}, u32[]{:S(2)}, u32[]{:S(2)}) collective-permute-start(f32[16,1024]{1,0:T(8,128)S(1)} %get-tuple-element.16), channel_id=1, source_target_pairs={{0,15},{1,0},{2,1},{3,2},{4,3},{5,4},{6,5},{7,6},{8,7},{9,8},{10,9... | collective-permute-start | bytes 196616 | tf_op jit(solution)/shard_map/ppermute | solution.py:268
  111.0 0.4 collective-permute-start.1
  111.4 2.2 %collective-permute-start.2 = (bf16[16,1024]{1,0:T(8,128)(2,1)S(1)}, bf16[16,1024]{1,0:T(8,128)(2,1)S(1)}, u32[]{:S(2)}, u32[]{:S(2)}) collective-permute-start(bf16[16,1024]{1,0:T(8,128)(2,1)S(1)} %get-tuple-element.14), channel_id=1, source_target_pairs={{0,7},{1,8},{2,9},{3,10},{4,11},{5,12},{6,13},{7,14},{8,15},{9,0},... | collective-permute-start | bytes 98312 | tf_op jit(solution)/shard_map/ppermute | solution.py:268
  113.6 0.0 copy-done
  113.6 0.1 copy.16.offsets_ref
  113.7 0.1 stack.39.place_ref
  113.8 1.4 %collective-permute-done.1.refs_0_ = bf16[16,1024]{1,0:T(8,128)(2,1)S(1)} collective-permute-done((bf16[16,1024]{1,0:T(8,128)(2,1)S(1)}, bf16[16,1024]{1,0:T(8,128)(2,1)S(1)}, u32[]{:S(2)}, u32[]{:S(2)}) %collective-permute-start.1) | collective-permute-done | bytes 32800 | tf_op jit(solution)/shard_map/ppermute | solution.py:268
  115.2 1.2 %collective-permute-done.2.refs_1_ = bf16[16,1024]{1,0:T(8,128)(2,1)S(1)} collective-permute-done((bf16[16,1024]{1,0:T(8,128)(2,1)S(1)}, bf16[16,1024]{1,0:T(8,128)(2,1)S(1)}, u32[]{:S(2)}, u32[]{:S(2)}) %collective-permute-start.2) | collective-permute-done | bytes 32800 | tf_op jit(solution)/shard_map/ppermute | solution.py:268
  116.4 0.0 collective-permute-done.3.refs_2_
  116.4 0.0 collective-permute-done.4.refs_3_
  116.4 0.0 collective-permute-done.other_ref
  116.4 3.4 %detect.1 = f32[8,64,2048]{2,1,0:T(8,128)} custom-call(s32[8,2]{1,0:T(8,128)S(1)} %copy.16.offsets_ref, s32[5]{0:T(128)S(1)} %stack.39.place_ref, bf16[64,2048]{1,0:T(8,128)(2,1)S(1)} %collective-permute-done.other_ref, f32[64,2048]{1,0:T(8,128)S(1)} %get-tuple-element.12.own_ref, bf16[16,1024]{1,0:T(8,128)(2,1)S(1)} %collective-permute-done.1.refs_0_, ...), custom_call_target="tpu_custom_call" | custom-call | flops 3145728 | bytes 4194304 | tf_op jit(solution)/shard_map/detect/pallas_call | solution.py:223
  (4 shorter events, 0.0 us)
Async XLA Ops:
  4.3 48.5 %all-to-all-start = ((bf16[16,4,64,256]{3,2,1,0:T(8,128)(2,1)}), bf16[16,4,64,256]{3,2,1,0:T(8,128)(2,1)S(1)}, u32[]{:S(2)}, u32[]{:S(2)}) async-start(bf16[16,4,64,256]{3,2,1,0:T(8,128)(2,1)} %pack.1), calls=%async_computation | async-start | bytes 4194304 | tf_op jit(solution)/shard_map/all_to_all | solution.py:261
  57.7 24.8 %all-to-all-start.1 = ((bf16[8,4,64,256]{3,2,1,0:T(8,128)(2,1)}), bf16[8,4,64,256]{3,2,1,0:T(8,128)(2,1)}, u32[]{:S(2)}, u32[]{:S(2)}) async-start(bf16[8,4,64,256]{3,2,1,0:T(8,128)(2,1)} %first_pass.2), calls=%async_computation.1 | async-start | bytes 2097152 | tf_op jit(solution)/shard_map/all_to_all | solution.py:265
  72.9 13.2 %copy-start.2 = (f32[2,3]{1,0:T(2,128)S(1)}, f32[2,3]{1,0:T(2,128)}, u32[]{:S(2)}) copy-start(f32[2,3]{1,0:T(2,128)} %param.14) | copy-start | bytes 76
  72.9 16.4 %copy-start.1 = (f32[1,3]{1,0:T(1,128)S(1)}, f32[1,3]{1,0:T(1,128)}, u32[]{:S(2)}) copy-start(f32[1,3]{1,0:T(1,128)} %constant.85) | copy-start | bytes 40
  82.6 18.0 %all-to-all-start.2 = ((bf16[8,4,64,256]{3,2,1,0:T(8,128)(2,1)}), bf16[8,4,64,256]{3,2,1,0:T(8,128)(2,1)S(1)}, u32[]{:S(2)}, u32[]{:S(2)}) async-start(bf16[8,4,64,256]{3,2,1,0:T(8,128)(2,1)} %first_pass.3), calls=%async_computation.2 | async-start | bytes 2097152 | tf_op jit(solution)/shard_map/all_to_all | solution.py:265
  95.9 17.7 %copy-start = (s32[8,2]{0,1:T(2,128)S(1)}, s32[8,2]{0,1:T(2,128)}, u32[]{:S(2)}) copy-start(s32[8,2]{0,1:T(2,128)} %param.15) | copy-start | bytes 196
  95.9 20.6 %collective-permute-start = (bf16[64,2048]{1,0:T(8,128)(2,1)S(1)}, bf16[64,2048]{1,0:T(8,128)(2,1)S(1)}, u32[]{:S(2)}, u32[]{:S(2)}) collective-permute-start(bf16[64,2048]{1,0:T(8,128)(2,1)S(1)} %get-tuple-element.11), channel_id=1, source_target_pairs={{0,8},{1,9},{2,10},{3,11},{4,12},{5,13},{6,14},{7,15},{8,0},{9,1},... | collective-permute-start | bytes 786440 | tf_op jit(solution)/shard_map/ppermute | solution.py:268
  106.5 10.0 %collective-permute-start.3 = (f32[16,1024]{1,0:T(8,128)S(1)}, f32[16,1024]{1,0:T(8,128)S(1)}, u32[]{:S(2)}, u32[]{:S(2)}) collective-permute-start(f32[16,1024]{1,0:T(8,128)S(1)} %get-tuple-element.15), channel_id=1, source_target_pairs={{0,1},{1,2},{2,3},{3,4},{4,5},{5,6},{6,7},{7,8},{8,9},{9,10},{10,1... | collective-permute-start | bytes 196616 | tf_op jit(solution)/shard_map/ppermute | solution.py:268
  106.5 9.9 %collective-permute-start.4 = (f32[16,1024]{1,0:T(8,128)S(1)}, f32[16,1024]{1,0:T(8,128)S(1)}, u32[]{:S(2)}, u32[]{:S(2)}) collective-permute-start(f32[16,1024]{1,0:T(8,128)S(1)} %get-tuple-element.16), channel_id=1, source_target_pairs={{0,15},{1,0},{2,1},{3,2},{4,3},{5,4},{6,5},{7,6},{8,7},{9,8},{10,9... | collective-permute-start | bytes 196616 | tf_op jit(solution)/shard_map/ppermute | solution.py:268
  111.0 4.2 %collective-permute-start.1 = (bf16[16,1024]{1,0:T(8,128)(2,1)S(1)}, bf16[16,1024]{1,0:T(8,128)(2,1)S(1)}, u32[]{:S(2)}, u32[]{:S(2)}) collective-permute-start(bf16[16,1024]{1,0:T(8,128)(2,1)S(1)} %get-tuple-element.13), channel_id=1, source_target_pairs={{0,9},{1,10},{2,11},{3,12},{4,13},{5,14},{6,15},{7,0},{8,1},{9,2},... | collective-permute-start | bytes 98312 | tf_op jit(solution)/shard_map/ppermute | solution.py:268
  111.4 5.0 %collective-permute-start.2 = (bf16[16,1024]{1,0:T(8,128)(2,1)S(1)}, bf16[16,1024]{1,0:T(8,128)(2,1)S(1)}, u32[]{:S(2)}, u32[]{:S(2)}) collective-permute-start(bf16[16,1024]{1,0:T(8,128)(2,1)S(1)} %get-tuple-element.14), channel_id=1, source_target_pairs={{0,7},{1,8},{2,9},{3,10},{4,11},{5,12},{6,13},{7,14},{8,15},{9,0},... | collective-permute-start | bytes 98312 | tf_op jit(solution)/shard_map/ppermute | solution.py:268

commit v3 on v2

v3 whole, which is shorter than its diff:
```python
import functools
import math

import jax
import jax.numpy as jnp
import numpy as np
from jax import lax
from jax.experimental import pallas as pl
from jax.experimental.pallas import tpu as pltpu
from jax.sharding import PartitionSpec as P

DMAX = 8
LANES = 128
BF16 = jnp.bfloat16
F32 = jnp.float32
SEG, LOWEST, TOP, FIRST, LAST = range(5)
SMEM = pl.BlockSpec(memory_space=pltpu.SMEM)
VMEM = pl.BlockSpec(memory_space=pltpu.VMEM)
ANY = pl.BlockSpec(memory_space=pl.ANY)


def params(mebibytes):
    return pltpu.CompilerParams(vmem_limit_bytes=mebibytes * 1024 * 1024)


def cost(flops, moved):
    return pl.CostEstimate(flops=flops, bytes_accessed=moved, transcendentals=0)


def dft_table(rows, cols, length):
    products = rows[:, None].astype(np.int64) * cols[None, :] % length
    angle = products.astype(np.float32) * np.float32(2.0 * math.pi / length)
    return np.cos(angle), -np.sin(angle)


def in_hbm(x):
    return pltpu.with_memory_space_constraint(x, pltpu.HBM)


def dot(x, y):
    return jnp.dot(x, y, preferred_element_type=F32)


def pack_kernel(x_ref, out_ref):
    cols = out_ref.shape[-1]
    for piece in range(out_ref.shape[0]):
        out_ref[piece] = x_ref[0, :, :, piece * cols : (piece + 1) * cols]


def pack(series, groups):
    segs, comps, rows, width = series.shape
    shape = (segs * groups, comps, rows, width // groups)
    return pl.pallas_call(
        pack_kernel,
        grid=(segs,),
        in_specs=[pl.BlockSpec((1, comps, rows, width), lambda s: (s, 0, 0, 0))],
        out_specs=pl.BlockSpec((groups,) + shape[1:], lambda s: (s, 0, 0, 0)),
        out_shape=pltpu.HBM(shape, BF16),
        compiler_params=params(16),
        cost_estimate=cost(0, 4 * math.prod(shape)),
        name="pack",
    )(in_hbm(series))


def first_kernel(half_ref, x_ref, sort_ref, wr_ref, wi_ref, br_ref, bi_ref, vr_ref, vi_ref, out_ref, sorted_ref):
    length = wr_ref.shape[1]
    comps, cols = x_ref.shape[1], x_ref.shape[-1]

    @pl.when(pl.program_id(0) == 0)
    def _():
        for comp in range(comps):
            sorted_ref[comp] = dot(x_ref[:, comp].reshape(length, cols), sort_ref[...]).astype(BF16)

    shape = (out_ref.shape[0],) + out_ref.shape[2:]
    by_real, by_imag = vr_ref[...], vi_ref[...]
    t_real = br_ref[...] * by_real - bi_ref[...] * by_imag
    t_imag = br_ref[...] * by_imag + bi_ref[...] * by_real
    for lead in range(0, comps, 2):
        x_real, x_imag = sorted_ref[lead], sorted_ref[lead + 1]
        real_part = dot(wr_ref[...], x_real) - dot(wi_ref[...], x_imag)
        imag_part = dot(wi_ref[...], x_real) + dot(wr_ref[...], x_imag)
        out_ref[:, lead] = (real_part * t_real - imag_part * t_imag).astype(BF16).reshape(shape)
        out_ref[:, lead + 1] = (real_part * t_imag + imag_part * t_real).astype(BF16).reshape(shape)


def first_pass(pieces, half, order, tables, bases, turns, groups):
    count, comps, rows, cols = pieces.shape
    length = count * rows
    per_half = groups * rows
    tile = min(256, per_half)
    steps = per_half // tile
    sort = np.zeros((cols, cols), np.float32)
    sort[order, np.arange(cols)] = 1.0
    strip = lambda width: pl.BlockSpec((tile, width), lambda t, half: (half[0] * steps + t, 0))
    return pl.pallas_call(
        first_kernel,
        grid_spec=pltpu.PrefetchScalarGridSpec(
            num_scalar_prefetch=1,
            grid=(steps,),
            in_specs=[VMEM, pl.BlockSpec((cols, cols), lambda t, half: (0, 0))]
            + [strip(length)] * 2
            + [strip(cols)] * 2
            + [strip(1)] * 2,
            out_specs=pl.BlockSpec((tile // rows, comps, rows, cols), lambda t, half: (t, 0, 0, 0)),
            scratch_shapes=[pltpu.VMEM((comps, length, cols), BF16)],
        ),
        out_shape=pltpu.HBM((groups, comps, rows, cols), BF16),
        compiler_params=params(24),
        cost_estimate=cost(4 * comps * per_half * length * cols, 4 * per_half * length),
        name="first_pass",
    )(half, pieces, in_hbm(sort.astype(BF16)), *map(in_hbm, tables), *map(in_hbm, bases), *turns)


def fstat_kernel(length, place_ref, coef_ref, z_ref, er_ref, ei_ref, or_ref, oi_ref, fstat_ref, lhs_ref):
    step = pl.program_id(0)

    @pl.when(step == 0)
    def _():
        groups, cols = z_ref.shape[0], z_ref.shape[-1] // 2
        for source in range(groups):
            piece = z_ref[source].reshape(lhs_ref.shape[1], 2 * cols)
            for parity in range(2):
                at = slice(source * cols, (source + 1) * cols)
                lhs_ref[parity, :, at] = piece[:, parity * cols : (parity + 1) * cols]

    rows, width = fstat_ref.shape
    tile = er_ref.shape[1]
    even, odd = lhs_ref[0], lhs_ref[1]
    even_real, even_imag = dot(even, er_ref[...]), dot(even, ei_ref[...])
    odd_real, odd_imag = dot(odd, or_ref[...]), dot(odd, oi_ref[...])
    coef_a, coef_b, coef_c = [jnp.full((1, tile), coef_ref[place_ref[SEG], at], F32) for at in range(3)]
    scale = 1.0 / ((coef_a * coef_b - coef_c * coef_c) * length)
    coef_a, coef_b, coef_c = coef_a * scale, coef_b * scale, 2.0 * coef_c * scale
    for half in range(2):
        by_real = even_real - odd_real if half else even_real + odd_real
        by_imag = even_imag - odd_imag if half else even_imag + odd_imag
        part = lambda x, comp: x[comp * rows : (comp + 1) * rows]
        a_real = part(by_real, 0) - part(by_imag, 1)
        a_imag = part(by_imag, 0) + part(by_real, 1)
        b_real = part(by_real, 2) - part(by_imag, 3)
        b_imag = part(by_imag, 2) + part(by_real, 3)
        fstat = (
            coef_b * (a_real * a_real + a_imag * a_imag)
            + coef_a * (b_real * b_real + b_imag * b_imag)
            - coef_c * (a_real * b_real + a_imag * b_imag)
        )
        at = pl.ds(pl.multiple_of(half * (width // 2) + step * tile, tile), tile)
        fstat_ref[:, at] = fstat.astype(fstat_ref.dtype)


def fstat_pass(z, place, tables, antenna, length, kind):
    groups, comps, rows, cols = z.shape
    width = groups * cols
    span = width // 2
    tile = min(256, span)
    return pl.pallas_call(
        functools.partial(fstat_kernel, length),
        grid=(span // tile,),
        in_specs=[SMEM, SMEM, VMEM] + [pl.BlockSpec((span, tile), lambda t: (0, t))] * 4,
        out_specs=pl.BlockSpec((rows, width), lambda t: (0, 0)),
        out_shape=jax.ShapeDtypeStruct((rows, width), kind),
        scratch_shapes=[pltpu.VMEM((2, comps * rows, span), BF16)],
        compiler_params=params(24),
        cost_estimate=cost(2 * comps * rows * width * width, 2 * width * width),
        name="fstat_pass",
    )(place, antenna, z, *map(in_hbm, tables))


def detect_kernel(offsets_ref, place_ref, other_ref, own_ref, lower_ref, upper_ref, out_ref, *wide_refs):
    rows = own_ref.shape[0]

    @pl.when(pl.program_id(0) == 0)
    def _():
        is_first, is_last, seg = place_ref[FIRST] == 1, place_ref[LAST] == 1, place_ref[SEG]
        lowest, top = place_ref[LOWEST] == 1, place_ref[TOP] == 1
        width = own_ref.shape[1]
        rims = [ref[...].astype(F32) for ref in (lower_ref, upper_ref)]
        first, second = [x[:DMAX] for x in rims], [x[DMAX:] for x in rims]

        def widen(wide_ref, middle, lower, upper):
            lower = jnp.where(is_first, pltpu.roll(lower, 1, 1), lower)
            upper = jnp.where(is_last, pltpu.roll(upper, width - 1, 1), upper)
            for strip in range(width // LANES):
                at = slice(strip * LANES, (strip + 1) * LANES)
                wide_ref[strip, :DMAX] = lower[:, at]
                wide_ref[strip, DMAX : DMAX + rows] = middle[:, at]
                wide_ref[strip, DMAX + rows :] = upper[:, at]

        def place(own_wide, other_wide):
            lower = jnp.where(lowest, second[0], first[0]), jnp.where(lowest, first[0], second[0])
            upper = jnp.where(top, second[1], first[1]), jnp.where(top, first[1], second[1])
            widen(own_wide, own_ref[...], lower[0], upper[0])
            widen(other_wide, other_ref[...].astype(F32), lower[1], upper[1])

        @pl.when(seg == 0)
        def _():
            place(wide_refs[0], wide_refs[1])

        @pl.when(seg != 0)
        def _():
            place(wide_refs[1], wide_refs[0])

    for at in range(out_ref.shape[0]):
        template = pl.program_id(0) * out_ref.shape[0] + at
        begins = [DMAX + offsets_ref[template, s] for s in range(len(wide_refs))]
        for strip in range(own_ref.shape[1] // LANES):
            total = wide_refs[0][strip, pl.ds(begins[0], rows), :]
            for begin, wide_ref in zip(begins[1:], wide_refs[1:]):
                total = total + wide_ref[strip, pl.ds(begin, rows), :]
            out_ref[at, :, strip * LANES : (strip + 1) * LANES] = total * (1.0 / len(wide_refs))


def detect(offsets, place, other, own, lower, upper):
    templates = offsets.shape[0]
    rows, width = own.shape
    batch = 2 - templates % 2
    return pl.pallas_call(
        detect_kernel,
        grid=(templates // batch,),
        in_specs=[SMEM, SMEM] + [VMEM] * 4,
        out_specs=pl.BlockSpec((batch, rows, width), lambda t: (t, 0, 0)),
        out_shape=jax.ShapeDtypeStruct((templates, rows, width), F32),
        scratch_shapes=[pltpu.VMEM((width // LANES, rows + 2 * DMAX, LANES), F32)] * 2,
        compiler_params=params(8),
        cost_estimate=cost(3 * templates * rows * width, 4 * templates * rows * width),
        name="detect",
    )(offsets, place, other, own, lower, upper)


def local(series, antenna, offsets):
    devices = lax.axis_size("tm")
    index = lax.axis_index("tm")
    segs, _, rows, width = series.shape
    slow = devices * rows
    length = slow * width
    groups = devices // segs
    cols = width // groups
    seg, member = index // groups, index % groups
    place = jnp.stack([seg, member == 0, member == groups - 1, index == 0, index == devices - 1]).astype(jnp.int32)

    bins = np.arange(slow)
    short = [x.astype(BF16) for x in dft_table(bins, bins, slow)]
    fast = np.arange(width // 2)
    long = [x.astype(BF16) for parity in range(2) for x in dft_table(2 * fast + parity, fast, width)]
    order = np.concatenate([np.arange(0, cols, 2), np.arange(1, cols, 2)])
    bases = dft_table(bins, order, length)
    angle = (jnp.arange(slow, dtype=jnp.int32) * (member * cols) % length).astype(F32) * (2.0 * math.pi / length)
    turns = (jnp.cos(angle)[:, None], -jnp.sin(angle)[:, None])

    halves = [[g * groups + i for i in range(groups)] for g in range(segs)]
    trade = functools.partial(lax.all_to_all, axis_name="tm", split_axis=0, concat_axis=0, tiled=True)
    pieces = trade(pack(series, groups))

    def rows_of(half):
        turned = first_pass(pieces, half[None], order, short, bases, turns, groups)
        return trade(turned, axis_index_groups=halves)

    def move(x, by):
        return lax.ppermute(x, "tm", [(i, (i + by) % devices) for i in range(devices)])

    far, near = rows_of(1 - seg), rows_of(seg)
    other = move(fstat_pass(far, place, long, antenna, length, BF16), groups)
    own = fstat_pass(near, place, long, antenna, length, F32)

    def rims(begin):
        at = slice(begin, begin + DMAX)
        return jnp.concatenate([own[at].astype(BF16), other[at]], axis=0)

    return detect(offsets, place, other, own, move(rims(rows - DMAX), 1), move(rims(0), -1))


def solution(mesh):
    return jax.shard_map(
        local,
        mesh=mesh,
        in_specs=(P("sky", None, "tm", None), P("sky", None), P("sky", None)),
        out_specs=P("sky", "tm", None),
        check_vma=False,
    )
```

time: 122 us -> 133 us (1.090); the launches traced: 120 us -> 133 us
  waiting for transfers between devices: 50.8 us -> 71.7 us
  starting transfers between devices: 31.6 us -> 26.8 us
  between operations: 2.67 us -> 0.12 us
    ppermute x5 -> x3, waiting for transfers between devices: 2.66 us -> 18 us  [move(): lax.ppermute(x, 'tm', [(i, (i + by) % devices) for i in range(devices)])]
    all_to_all x2, waiting for transfers between devices: 11 us -> 16.5 us  [rows_of(): return trade(turned, axis_index_groups=halves)]
    ppermute x5 -> x3, starting transfers between devices: 10.4 us -> 5.54 us  [move(): lax.ppermute(x, 'tm', [(i, (i + by) % devices) for i in range(devices)])]
    pallas_call x2, Pallas kernels: 9.82 us -> 11.6 us  [first_pass(): pl.pallas_call(first_kernel, grid_spec=pltpu.PrefetchScalarGridSpec(num_s...]
    pallas_call x3, Pallas kernels: 16.8 us -> 15 us  [the longest x2 12.4 us: fstat_pass(): pl.pallas_call(functools.partial(fstat_kernel, length), grid=(span // til...]
  transfers between devices with their start and end apart: 8 -> 6, of which waited for: 5 -> 6; matrix products, arithmetic and copies ran while one was open for 4% -> 3% of each run, Pallas kernels for 14% -> 9%
where the time goes in v3:
time: 133 us
  waiting for transfers between devices  71.7 us (54%)
  Pallas kernels  30 us (23%)
  starting transfers between devices  26.8 us (20%)
  other arithmetic  2.89 us (2%)
    all_to_all x1, waiting for transfers between devices, local(): pieces = trade(pack(series, groups))  37.2 us
    ppermute x3, waiting for transfers between devices, move(): lax.ppermute(x, 'tm', [(i, (i + by) % devices) for i in range(devices)])  18 us
    all_to_all x2, waiting for transfers between devices, rows_of(): return trade(turned, axis_index_groups=halves)  16.5 us
    all_to_all x2, starting transfers between devices, rows_of(): return trade(turned, axis_index_groups=halves)  13.8 us
    pallas_call x2, Pallas kernels, fstat_pass(): pl.pallas_call(functools.partial(fstat_kernel, length), grid=(span // til...  12.4 us
    pallas_call x2, Pallas kernels, first_pass(): pl.pallas_call(first_kernel, grid_spec=pltpu.PrefetchScalarGridSpec(num_s...  11.6 us
    all_to_all x1, starting transfers between devices, local(): pieces = trade(pack(series, groups))  7.39 us
    ppermute x3, starting transfers between devices, move(): lax.ppermute(x, 'tm', [(i, (i + by) % devices) for i in range(devices)])  5.54 us
  transfers between devices with their start and end apart: 6, of which 6 were waited for; matrix products, arithmetic and copies ran while one was open for 3% of the time, Pallas kernels for 9%

profile of v3, /device:TPU:0, one launch (start us, length us, event | category | flops | bytes accessed | tf_op | source)
XLA Modules:
  0.0 132.7 jit_solution(12319245989663921700)
XLA Ops:
  0.0 2.6 %pack.1 = bf16[16,4,64,256]{3,2,1,0:T(8,128)(2,1)} custom-call(bf16[2,4,64,2048]{3,2,1,0:T(8,128)(2,1)} %x_ref.1), custom_call_target="tpu_custom_call" | custom-call | bytes 4194304 | tf_op jit(solution)/shard_map/pack/pallas_call | solution.py:53
  2.6 7.4 %all-to-all-start = ((bf16[16,4,64,256]{3,2,1,0:T(8,128)(2,1)}), bf16[16,4,64,256]{3,2,1,0:T(8,128)(2,1)S(1)}, u32[]{:S(2)}, u32[]{:S(2)}) async-start(bf16[16,4,64,256]{3,2,1,0:T(8,128)(2,1)} %pack.1), calls=%async_computation | async-start | bytes 4194304 | tf_op jit(solution)/shard_map/all_to_all | solution.py:252
  10.1 1.0 copy.15
  11.1 2.8 %sine_negate_fusion = (f32[1024,1]{1,0:T(8,128)S(1)}, f32[1024,1]{1,0:T(8,128)S(1)}) fusion(f32[1024,1]{1,0:T(8,128)} %copy.15), kind=kLoop, calls=%fused_computation | loop fusion | flops 2048 | bytes 12288 | tf_op jit(solution)/shard_map/neg | solution.py:248
  13.9 37.2 %all-to-all-done.x_ref = bf16[16,4,64,256]{3,2,1,0:T(8,128)(2,1)S(1)} async-done(((bf16[16,4,64,256]{3,2,1,0:T(8,128)(2,1)}), bf16[16,4,64,256]{3,2,1,0:T(8,128)(2,1)S(1)}, u32[]{:S(2)}, u32[]{:S(2)}) %all-to-all-start) | async-done | bytes 2097184 | tf_op jit(solution)/shard_map/all_to_all | solution.py:252
  51.1 5.8 %first_pass.3 = bf16[8,4,64,256]{3,2,1,0:T(8,128)(2,1)} custom-call(s32[1]{0:T(128)} %bitcast.half_ref, bf16[16,4,64,256]{3,2,1,0:T(8,128)(2,1)S(1)} %all-to-all-done.x_ref, bf16[256,256]{1,0:T(8,128)(2,1)} %constant.67.clone.sort_ref, bf16[1024,1024]{1,0:T(8,128)(2,1)} %constant.68.clone.wr_ref.er_ref, bf16[1024,1024]{1,0:T(8,128)(2,1)} %constant.69.clone.wi_ref.ei_ref, ...), custom_call_target="tpu_custom_call" | custom-call | flops 2147483648 | bytes 2097152 | tf_op jit(solution)/shard_map/first_pass/pallas_call | solution.py:95
  56.9 10.3 %all-to-all-start.2 = ((bf16[8,4,64,256]{3,2,1,0:T(8,128)(2,1)}), bf16[8,4,64,256]{3,2,1,0:T(8,128)(2,1)}, u32[]{:S(2)}, u32[]{:S(2)}) async-start(bf16[8,4,64,256]{3,2,1,0:T(8,128)(2,1)} %first_pass.3), calls=%async_computation.2 | async-start | bytes 2097152 | tf_op jit(solution)/shard_map/all_to_all | solution.py:256
  67.2 5.8 %first_pass.2 = bf16[8,4,64,256]{3,2,1,0:T(8,128)(2,1)} custom-call(s32[1]{0:T(128)} %bitcast.5.half_ref, bf16[16,4,64,256]{3,2,1,0:T(8,128)(2,1)S(1)} %all-to-all-done.x_ref, bf16[256,256]{1,0:T(8,128)(2,1)} %constant.67.clone.sort_ref, bf16[1024,1024]{1,0:T(8,128)(2,1)} %constant.68.clone.wr_ref.er_ref, bf16[1024,1024]{1,0:T(8,128)(2,1)} %constant.69.clone.wi_ref.ei_ref, ...), custom_call_target="tpu_custom_call" | custom-call | flops 2147483648 | bytes 2097152 | tf_op jit(solution)/shard_map/first_pass/pallas_call | solution.py:95
  73.0 0.0 copy-start
  73.0 8.8 %all-to-all-done.2.z_ref = bf16[8,4,64,256]{3,2,1,0:T(8,128)(2,1)} async-done(((bf16[8,4,64,256]{3,2,1,0:T(8,128)(2,1)}), bf16[8,4,64,256]{3,2,1,0:T(8,128)(2,1)}, u32[]{:S(2)}, u32[]{:S(2)}) %all-to-all-start.2) | async-done | bytes 1048608 | tf_op jit(solution)/shard_map/all_to_all | solution.py:256
  81.7 3.6 %all-to-all-start.1 = ((bf16[8,4,64,256]{3,2,1,0:T(8,128)(2,1)}), bf16[8,4,64,256]{3,2,1,0:T(8,128)(2,1)S(1)}, u32[]{:S(2)}, u32[]{:S(2)}) async-start(bf16[8,4,64,256]{3,2,1,0:T(8,128)(2,1)} %first_pass.2), calls=%async_computation.1 | async-start | bytes 2097152 | tf_op jit(solution)/shard_map/all_to_all | solution.py:256
  85.3 0.1 stack.39.place_ref
  85.4 0.0 copy-done
  85.4 6.5 %fstat_pass.3.own_ref = f32[64,2048]{1,0:T(8,128)S(1)} custom-call(s32[5]{0:T(128)S(1)} %stack.39.place_ref, f32[2,3]{1,0:T(2,128)S(1)} %copy-done, bf16[8,4,64,256]{3,2,1,0:T(8,128)(2,1)} %all-to-all-done.2.z_ref, bf16[1024,1024]{1,0:T(8,128)(2,1)} %constant.68.clone.wr_ref.er_ref, bf16[1024,1024]{1,0:T(8,128)(2,1)} %constant.69.clone.wi_ref.ei_ref, ...), custom_call_target="tpu_custom_call" | custom-call | flops 2147483648 | bytes 8388608 | tf_op jit(solution)/shard_map/fstat_pass/pallas_call | solution.py:156
  91.9 0.0 copy-start.1
  91.9 7.7 %all-to-all-done.1.z_ref = bf16[8,4,64,256]{3,2,1,0:T(8,128)(2,1)S(1)} async-done(((bf16[8,4,64,256]{3,2,1,0:T(8,128)(2,1)}), bf16[8,4,64,256]{3,2,1,0:T(8,128)(2,1)S(1)}, u32[]{:S(2)}, u32[]{:S(2)}) %all-to-all-start.1) | async-done | bytes 1048608 | tf_op jit(solution)/shard_map/all_to_all | solution.py:256
  99.7 5.9 %fstat_pass.2 = bf16[64,2048]{1,0:T(8,128)(2,1)S(1)} custom-call(s32[5]{0:T(128)S(1)} %stack.39.place_ref, f32[2,3]{1,0:T(2,128)S(1)} %copy-done, bf16[8,4,64,256]{3,2,1,0:T(8,128)(2,1)S(1)} %all-to-all-done.1.z_ref, bf16[1024,1024]{1,0:T(8,128)(2,1)} %constant.68.clone.wr_ref.er_ref, bf16[1024,1024]{1,0:T(8,128)(2,1)} %constant.69.clone.wi_ref.ei_ref, ...), custom_call_target="tpu_custom_call" | custom-call | flops 2147483648 | bytes 8388608 | tf_op jit(solution)/shard_map/fstat_pass/pallas_call | solution.py:156
  105.6 3.3 %collective-permute-start = (bf16[64,2048]{1,0:T(8,128)(2,1)S(1)}, bf16[64,2048]{1,0:T(8,128)(2,1)S(1)}, u32[]{:S(2)}, u32[]{:S(2)}) collective-permute-start(bf16[64,2048]{1,0:T(8,128)(2,1)S(1)} %fstat_pass.2), channel_id=1, source_target_pairs={{0,8},{1,9},{2,10},{3,11},{4,12},{5,13},{6,14},{7,15},{8,0},{9,1},... | collective-permute-start | bytes 786440 | tf_op jit(solution)/shard_map/ppermute | solution.py:259
  109.0 11.7 %collective-permute-done.other_ref = bf16[64,2048]{1,0:T(8,128)(2,1)S(1)} collective-permute-done((bf16[64,2048]{1,0:T(8,128)(2,1)S(1)}, bf16[64,2048]{1,0:T(8,128)(2,1)S(1)}, u32[]{:S(2)}, u32[]{:S(2)}) %collective-permute-start) | collective-permute-done | bytes 262176 | tf_op jit(solution)/shard_map/ppermute | solution.py:259
  120.7 2.2 %collective-permute-start.2 = (bf16[16,2048]{1,0:T(8,128)(2,1)S(1)}, bf16[16,2048]{1,0:T(8,128)(2,1)S(1)}, u32[]{:S(2)}, u32[]{:S(2)}) collective-permute-start(bf16[16,2048]{1,0:T(8,128)(2,1)S(1)} %pad_maximum_fusion.1), channel_id=1, source_target_pairs={{0,15},{1,0},{2,1},{3,2},{4,3},{5,4},{6,5},{7,6},{8,7},{9,8},{10,9... | collective-permute-start | bytes 196616 | tf_op jit(solution)/shard_map/ppermute | solution.py:259
  122.9 0.0 collective-permute-start.1
  122.9 0.0 copy-done.1
  122.9 0.1 copy.16.offsets_ref
  123.0 1.8 %collective-permute-done.2.upper_ref = bf16[16,2048]{1,0:T(8,128)(2,1)S(1)} collective-permute-done((bf16[16,2048]{1,0:T(8,128)(2,1)S(1)}, bf16[16,2048]{1,0:T(8,128)(2,1)S(1)}, u32[]{:S(2)}, u32[]{:S(2)}) %collective-permute-start.2) | collective-permute-done | bytes 65568 | tf_op jit(solution)/shard_map/ppermute | solution.py:259
  124.8 4.5 %collective-permute-done.1.lower_ref = bf16[16,2048]{1,0:T(8,128)(2,1)S(1)} collective-permute-done((bf16[16,2048]{1,0:T(8,128)(2,1)S(1)}, bf16[16,2048]{1,0:T(8,128)(2,1)S(1)}, u32[]{:S(2)}, u32[]{:S(2)}) %collective-permute-start.1) | collective-permute-done | bytes 65568 | tf_op jit(solution)/shard_map/ppermute | solution.py:259
  129.3 3.4 %detect.1 = f32[8,64,2048]{2,1,0:T(8,128)} custom-call(s32[8,2]{1,0:T(8,128)S(1)} %copy.16.offsets_ref, s32[5]{0:T(128)S(1)} %stack.39.place_ref, bf16[64,2048]{1,0:T(8,128)(2,1)S(1)} %collective-permute-done.other_ref, f32[64,2048]{1,0:T(8,128)S(1)} %fstat_pass.3.own_ref, bf16[16,2048]{1,0:T(8,128)(2,1)S(1)} %collective-permute-done.1.lower_ref, ...), custom_call_target="tpu_custom_call" | custom-call | flops 3145728 | bytes 4194304 | tf_op jit(solution)/shard_map/detect/pallas_call | solution.py:217
  (6 shorter events, 0.1 us)
Async XLA Ops:
  2.6 48.5 %all-to-all-start = ((bf16[16,4,64,256]{3,2,1,0:T(8,128)(2,1)}), bf16[16,4,64,256]{3,2,1,0:T(8,128)(2,1)S(1)}, u32[]{:S(2)}, u32[]{:S(2)}) async-start(bf16[16,4,64,256]{3,2,1,0:T(8,128)(2,1)} %pack.1), calls=%async_computation | async-start | bytes 4194304 | tf_op jit(solution)/shard_map/all_to_all | solution.py:252
  56.9 24.8 %all-to-all-start.2 = ((bf16[8,4,64,256]{3,2,1,0:T(8,128)(2,1)}), bf16[8,4,64,256]{3,2,1,0:T(8,128)(2,1)}, u32[]{:S(2)}, u32[]{:S(2)}) async-start(bf16[8,4,64,256]{3,2,1,0:T(8,128)(2,1)} %first_pass.3), calls=%async_computation.2 | async-start | bytes 2097152 | tf_op jit(solution)/shard_map/all_to_all | solution.py:256
  73.0 12.4 %copy-start = (f32[2,3]{1,0:T(2,128)S(1)}, f32[2,3]{1,0:T(2,128)}, u32[]{:S(2)}) copy-start(f32[2,3]{1,0:T(2,128)} %coef_ref.3) | copy-start | bytes 76
  81.7 17.9 %all-to-all-start.1 = ((bf16[8,4,64,256]{3,2,1,0:T(8,128)(2,1)}), bf16[8,4,64,256]{3,2,1,0:T(8,128)(2,1)S(1)}, u32[]{:S(2)}, u32[]{:S(2)}) async-start(bf16[8,4,64,256]{3,2,1,0:T(8,128)(2,1)} %first_pass.2), calls=%async_computation.1 | async-start | bytes 2097152 | tf_op jit(solution)/shard_map/all_to_all | solution.py:256
  91.9 31.0 %copy-start.1 = (s32[8,2]{0,1:T(2,128)S(1)}, s32[8,2]{0,1:T(2,128)}, u32[]{:S(2)}) copy-start(s32[8,2]{0,1:T(2,128)} %param.15) | copy-start | bytes 196
  105.6 15.0 %collective-permute-start = (bf16[64,2048]{1,0:T(8,128)(2,1)S(1)}, bf16[64,2048]{1,0:T(8,128)(2,1)S(1)}, u32[]{:S(2)}, u32[]{:S(2)}) collective-permute-start(bf16[64,2048]{1,0:T(8,128)(2,1)S(1)} %fstat_pass.2), channel_id=1, source_target_pairs={{0,8},{1,9},{2,10},{3,11},{4,12},{5,13},{6,14},{7,15},{8,0},{9,1},... | collective-permute-start | bytes 786440 | tf_op jit(solution)/shard_map/ppermute | solution.py:259
  120.7 4.1 %collective-permute-start.2 = (bf16[16,2048]{1,0:T(8,128)(2,1)S(1)}, bf16[16,2048]{1,0:T(8,128)(2,1)S(1)}, u32[]{:S(2)}, u32[]{:S(2)}) collective-permute-start(bf16[16,2048]{1,0:T(8,128)(2,1)S(1)} %pad_maximum_fusion.1), channel_id=1, source_target_pairs={{0,15},{1,0},{2,1},{3,2},{4,3},{5,4},{6,5},{7,6},{8,7},{9,8},{10,9... | collective-permute-start | bytes 196616 | tf_op jit(solution)/shard_map/ppermute | solution.py:259
  122.9 6.4 %collective-permute-start.1 = (bf16[16,2048]{1,0:T(8,128)(2,1)S(1)}, bf16[16,2048]{1,0:T(8,128)(2,1)S(1)}, u32[]{:S(2)}, u32[]{:S(2)}) collective-permute-start(bf16[16,2048]{1,0:T(8,128)(2,1)S(1)} %pad_maximum_fusion), channel_id=1, source_target_pairs={{0,1},{1,2},{2,3},{3,4},{4,5},{5,6},{6,7},{7,8},{8,9},{9,10},{10,1... | collective-permute-start | bytes 196616 | tf_op jit(solution)/shard_map/ppermute | solution.py:259
